TPU v7x, 32 devices: a whole 2x2x4 slice. The times are simulated.
32 devices in a mesh: dp: 16 (over z, x, core), sp: 2 (over y).
Axes of the slice: x: 2, y: 2, z: 4, core: 2. Of those that a mesh axis runs over, the one named last changes fastest.
Arguments:
- features: bfloat16 [64, 32, 32, 128], P('dp', 'sp'), may hold values from -6 to 6
- target: bfloat16 [64, 32, 32, 3], P('dp', 'sp'), may hold values from -6 to 6
- pixel_mask: int32 [64, 32, 32], P('dp', 'sp'), may hold values from 0 to 1, as said below
- buckets: int32 [64], P('dp'), may hold values from 0 to 7
- conv_pair: float32 [2, 3, 3, 128, 128], replicated, may hold values from -0.1875 to 0.1875
- down_conv: float32 [3, 3, 128, 256], replicated, may hold values from -0.1875 to 0.1875
- conv_wide: float32 [3, 3, 256, 256], replicated, may hold values from -0.125 to 0.125
- skip_proj: float32 [128, 256], replicated, may hold values from -0.5 to 0.5
- attn_proj: float32 [256, 1024], replicated, may hold values from -0.375 to 0.375
- head_conv: float32 [3, 3, 256, 3], replicated, may hold values from -0.125 to 0.125
- norm_narrow: float32 [6, 128], replicated
- norm_wide: float32 [6, 256], replicated
- time_bias: float32 [8, 384], replicated, may hold values from -3 to 3
- conv_pair_mom: float32 [2, 3, 3, 128, 128], replicated, may hold values from -0.078125 to 0.078125
- down_conv_mom: float32 [3, 3, 128, 256], replicated, may hold values from -0.078125 to 0.078125
- conv_wide_mom: float32 [3, 3, 256, 256], replicated, may hold values from -0.078125 to 0.078125
- skip_proj_mom: float32 [128, 256], replicated, may hold values from -0.078125 to 0.078125
- attn_proj_mom: float32 [256, 1024], replicated, may hold values from -0.078125 to 0.078125
- head_conv_mom: float32 [3, 3, 256, 3], replicated, may hold values from -0.078125 to 0.078125
- norm_narrow_mom: float32 [6, 128], replicated, may hold values from -0.078125 to 0.078125
- norm_wide_mom: float32 [6, 256], replicated, may hold values from -0.078125 to 0.078125
- time_bias_mom: float32 [8, 384], replicated, may hold values from -0.078125 to 0.078125
- conv_pair_sq: float32 [2, 3, 3, 128, 128], replicated, as said below
- down_conv_sq: float32 [3, 3, 128, 256], replicated, as said below
- conv_wide_sq: float32 [3, 3, 256, 256], replicated, as said below
- skip_proj_sq: float32 [128, 256], replicated, as said below
- attn_proj_sq: float32 [256, 1024], replicated, as said below
- head_conv_sq: float32 [3, 3, 256, 3], replicated, as said below
- norm_narrow_sq: float32 [6, 128], replicated, as said below
- norm_wide_sq: float32 [6, 256], replicated, as said below
- time_bias_sq: float32 [8, 384], replicated, as said below
Outputs:
- loss_sum: float32 [], replicated
- bucket_counts: float32 [8], replicated
- conv_pair_new: float32 [2, 3, 3, 128, 128], replicated
- conv_pair_mom_new: float32 [2, 3, 3, 128, 128], replicated
- conv_pair_sq_new: float32 [2, 3, 3, 128, 128], replicated
- down_conv_new: float32 [3, 3, 128, 256], replicated
- down_conv_mom_new: float32 [3, 3, 128, 256], replicated
- down_conv_sq_new: float32 [3, 3, 128, 256], replicated
- conv_wide_new: float32 [3, 3, 256, 256], replicated
- conv_wide_mom_new: float32 [3, 3, 256, 256], replicated
- conv_wide_sq_new: float32 [3, 3, 256, 256], replicated
- skip_proj_new: float32 [128, 256], replicated
- skip_proj_mom_new: float32 [128, 256], replicated
- skip_proj_sq_new: float32 [128, 256], replicated
- attn_proj_new: float32 [256, 1024], replicated
- attn_proj_mom_new: float32 [256, 1024], replicated
- attn_proj_sq_new: float32 [256, 1024], replicated
- head_conv_new: float32 [3, 3, 256, 3], replicated
- head_conv_mom_new: float32 [3, 3, 256, 3], replicated
- head_conv_sq_new: float32 [3, 3, 256, 3], replicated
- norm_narrow_new: float32 [6, 128], replicated
- norm_narrow_mom_new: float32 [6, 128], replicated
- norm_narrow_sq_new: float32 [6, 128], replicated
- norm_wide_new: float32 [6, 256], replicated
- norm_wide_mom_new: float32 [6, 256], replicated
- norm_wide_sq_new: float32 [6, 256], replicated
- time_bias_new: float32 [8, 384], replicated
- time_bias_mom_new: float32 [8, 384], replicated
- time_bias_sq_new: float32 [8, 384], replicated
Inputs may be any that keep to these rules, and one draw needn't show every extreme that they name: `pixel_mask`: every row of every image has at least one pixel that counts. `conv_pair_sq`: positive. `down_conv_sq`: positive. `conv_wide_sq`: positive. `skip_proj_sq`: positive. `attn_proj_sq`: positive. `head_conv_sq`: positive. `norm_narrow_sq`: positive. `norm_wide_sq`: positive. `time_bias_sq`: positive.
All inputs are finite; a program needn't handle non-finite values.
Results may differ from a plain program's by a relative error of at most 0.0013.
The roundings to bfloat16 on the way count: a program that leaves them out, or rounds other values in their place, can miss the bound.
Values may be sent and summed in bfloat16 or wider, within the bound.
A program may use at most 128 MiB of HBM per device.

v0:
```python
import functools

import jax
import jax.numpy as jnp
from jax import lax
from jax.experimental import pallas as pl
from jax.experimental.pallas import tpu as pltpu
from jax.sharding import PartitionSpec as P

C1 = 128
HALF_CHANNELS = 256
GROUPS = 32
RES = 32
HALF = 16
NB = 8
STEP = 10
MESH = pl.DeviceIdType.MESH
VMEM_LIMIT = 62 * 1024 * 1024

epsilon = 1e-05
root_half = 0.7071067811865476
beta_one = 0.9
beta_two = 0.999
adam_epsilon = 1e-08
decay_rate = 0.1
rate_matrix = 0.03
rate_vector = 0.5
logit_scale = HALF_CHANNELS ** (-0.5)
ROWS = 8

bf16 = jnp.bfloat16
f32 = jnp.float32

EVEN, ODD, ODD_LEFT, EVEN_RIGHT = 0, 1, 2, 3
TAPS = ((ODD_LEFT, EVEN, ODD), (EVEN, ODD, EVEN_RIGHT))


def rounded(v):
    return v.astype(bf16).astype(f32)


def silu(t):
    return t * jax.nn.sigmoid(t)


def slope(t):
    s = jax.nn.sigmoid(t)
    return s * (1.0 + t * (1.0 - s))


def mm(a, b):
    return lax.dot_general(a, b, (((1,), (0,)), ((), ())), preferred_element_type=f32)


def mm_nt(a, b):
    return lax.dot_general(a, b, (((1,), (1,)), ((), ())), preferred_element_type=f32)


def mm_tn(a, b):
    return lax.dot_general(a, b, (((0,), (0,)), ((), ())), preferred_element_type=f32)


def fold(v):
    return jnp.sum(v.reshape(-1, 8, v.shape[-1]), axis=0)


def total(v):
    return jnp.broadcast_to(jnp.sum(v, axis=0, keepdims=True), v.shape)


def group_sum(v, size):
    lanes = v.shape[-1]
    lane = lax.broadcasted_iota(jnp.int32, v.shape, 1)
    step = 1
    while step < size:
        other = jnp.where(
            (lane & step) == 0, pltpu.roll(v, lanes - step, 1), pltpu.roll(v, step, 1)
        )
        v = v + other
        step *= 2
    return v


def norm_coefs(sums, squares, gain, shift, pixels):
    size = sums.shape[-1] // GROUPS
    count = pixels * size
    mean = group_sum(total(sums), size) / count
    power = group_sum(total(squares), size) / count
    inv = lax.rsqrt(power - mean * mean + epsilon)
    scale = inv * gain
    return scale, shift - mean * scale, mean, inv


def norm_grad_coefs(sum_dy, sum_dyv, gain, mean, inv, pixels):
    size = sum_dy.shape[-1] // GROUPS
    count = pixels * size
    first = total(sum_dy)
    second = (total(sum_dyv) - mean * first) * inv
    one = group_sum(first * gain, size) / count
    two = group_sum(second * gain, size) / count
    b = -inv * inv * two
    return second, first, inv * gain, b, -inv * one - mean * b


def shift_cols(v, step):
    col = lax.broadcasted_iota(jnp.int32, v.shape, 1)
    if step == 1:
        return jnp.where(col == 0, 0.0, pltpu.roll(v, 1, 1))
    return jnp.where(col == HALF - 1, 0.0, pltpu.roll(v, HALF - 1, 1))


def store_planes(planes, n, b, r0, v):
    rows = v.shape[0]
    v = v.astype(bf16).astype(f32)
    for plane, value in (
        (EVEN + b, v),
        (ODD_LEFT if b == 1 else EVEN_RIGHT, shift_cols(v, 1 if b == 1 else -1)),
    ):
        planes[n, plane, pl.ds(r0 + 1, rows)] = value.astype(bf16)


def store_shifted(cells, n, r0, v):
    rows = v.shape[0]
    v = v.astype(bf16).astype(f32)
    for tap, value in ((0, shift_cols(v, 1)), (1, v), (2, shift_cols(v, -1))):
        cells[n, tap, pl.ds(r0 + 1, rows)] = value.astype(bf16)


def plane_block(planes, tap, jj):
    return planes[:, tap, pl.ds(jj, HALF, stride=2)].reshape(-1, planes.shape[-1])


def pair_input(planes, b, jjs):
    return jnp.concatenate([plane_block(planes, tap, jj) for jj in jjs for tap in TAPS[b]], axis=1)


def cell_input(cells, dys):
    return jnp.concatenate(
        [
            cells[:, tap, dy : dy + HALF].reshape(-1, cells.shape[-1])
            for dy in dys
            for tap in range(3)
        ],
        axis=1,
    )


def each(count, body):
    def step(i, carry):
        body(i)
        return carry

    lax.fori_loop(0, count, step, 0)


def prepare_weights(pair, down, wide, skip, attn, head, pair_fwd, pair_bwd, down_fwd, down_bwd, wide_fwd, wide_bwd, skip_low, attn_low, head_low):
    nothing = jnp.zeros((C1, C1), bf16)
    for member in range(2):
        for jj in range(4):
            for k in range(3):
                block = (jj * 3 + k) * C1
                for a in range(2):
                    dy = jj - a
                    inside = 0 <= dy < 3
                    row = (member * 9 + dy * 3 + k) * C1
                    back = (member * 9 + (2 - dy) * 3 + (2 - k)) * C1
                    pair_fwd[member, block : block + C1, a * C1 : a * C1 + C1] = (
                        pair[row : row + C1, :].astype(bf16) if inside else nothing
                    )
                    pair_bwd[member, a * C1 : a * C1 + C1, block : block + C1] = (
                        pair[back : back + C1, :].astype(bf16) if inside else nothing
                    )
    wide_channels = HALF_CHANNELS
    for tap in range(9):
        low = down[tap * C1 : tap * C1 + C1, :].astype(bf16)
        down_fwd[tap * C1 : tap * C1 + C1, :] = low
        down_bwd[:, (8 - tap) * wide_channels : (9 - tap) * wide_channels] = low
        low = wide[tap * wide_channels : (tap + 1) * wide_channels, :].astype(bf16)
        wide_fwd[tap * wide_channels : (tap + 1) * wide_channels, :] = low
        wide_bwd[:, (8 - tap) * wide_channels : (9 - tap) * wide_channels] = low
    skip_low[...] = skip[...].astype(bf16)
    attn_low[...] = attn[...].astype(bf16)
    head_low[...] = jnp.zeros(head_low.shape, f32)
    for tap in range(9):
        head_low[tap * 8 : tap * 8 + 3, :] = rounded(head[tap])


def split_three(v):
    high = v.astype(bf16)
    rest = v - high.astype(f32)
    middle = rest.astype(bf16)
    return high, middle, (rest - middle.astype(f32)).astype(bf16)


def lane_shift(v, step):
    lane = lax.broadcasted_iota(jnp.int32, v.shape, 1)
    j = lane & (HALF - 1)
    if step == 1:
        keep = j < HALF - 1
    elif step == -1:
        keep = j > 0
    elif step == HALF:
        keep = lane < HALF * (HALF - 1)
    else:
        keep = lane >= HALF
    return jnp.where(keep, pltpu.roll(v, (-step) % v.shape[-1], 1), 0.0)


def head_forward(table):
    cols = [
        [
            lane_shift(table[dy][0], -1) + table[dy][1] + table[dy][2],
            table[dy][0] + table[dy][1] + lane_shift(table[dy][2], 1),
        ]
        for dy in range(3)
    ]
    return [
        [
            lane_shift(cols[0][b], -HALF) + cols[1][b] + cols[2][b]
            if a == 0
            else cols[0][b] + cols[1][b] + lane_shift(cols[2][b], HALF)
            for b in range(2)
        ]
        for a in range(2)
    ]


def head_backward(grad):
    rows = [
        [
            lane_shift(grad[0][b], HALF) + grad[1][b],
            grad[0][b] + grad[1][b],
            grad[0][b] + lane_shift(grad[1][b], -HALF),
        ]
        for b in range(2)
    ]
    return [
        [
            lane_shift(rows[0][dy], 1) + rows[1][dy],
            rows[0][dy] + rows[1][dy],
            rows[0][dy] + lane_shift(rows[1][dy], -1),
        ]
        for dy in range(3)
    ]


def keep_columns(ref, row, v):
    for c in range(v.shape[1] // 128):
        ref[row + c * v.shape[0] : row + (c + 1) * v.shape[0], :] = v[:, c * 128 : (c + 1) * 128]


HEAD_ROWS = 72
WIDE_NORM_ROW = 72
LOSS_ROW = 78
NARROW_NORM_ROW = 80
TIME_WIDE_ROW = 88
TIME_NARROW_ROW = 96
SMALL_ROWS = 128
SKIP_ROW = 18 * C1
PIECES = (
    (8 * HALF_CHANNELS, 128),
    (18 * HALF_CHANNELS, 128),
    (20 * C1, 128),
    (18 * C1, 128),
    (SMALL_ROWS, HALF_CHANNELS),
)


def main_kernel(
    buckets, x_in, target, mask, counts, pair, down, wide, skip, attn, head, gains_narrow, gains_wide, time_bias,
    g_attn, g_wide, g_down, g_pair, g_small,
    pair_fwd, pair_bwd, down_fwd, down_bwd, wide_fwd, wide_bwd, skip_low, attn_low, head_low,
    x_full, h1_full, xs_full, dy_full, in_a, in_b, in_g, flat,
    cells_c, cells_d, cells_g, fs_low, dfs, h3, x2, x3, n5, qkv, probs, probs_low, att, a6, dwide, dout, dqkv, dnarrow,
    coef_n, coef_w,
):
    images = x_in.shape[1]
    position = lax.axis_index("sp")
    steps = RES // ROWS
    full_pixels = RES * RES
    half_pixels = HALF * HALF
    zero_n = jnp.zeros((8, C1), f32)
    zero_w = jnp.zeros((8, HALF_CHANNELS), f32)

    def bucket(n):
        return buckets[position * images + n]

    def gain_n(row):
        return jnp.broadcast_to(gains_narrow[row : row + 1, :], (8, C1))

    def gain_w(row):
        return jnp.broadcast_to(gains_wide[row : row + 1, :], (8, HALF_CHANNELS))

    def keep_coefs(ref, which, n, values):
        for kind in range(4):
            ref[which, n, kind] = values[kind]

    def row_of(ref, which, n, kind):
        return ref[which, n, kind, 0:1, :]

    prepare_weights(pair, down, wide, skip, attn, head, pair_fwd, pair_bwd, down_fwd, down_bwd, wide_fwd, wide_bwd, skip_low, attn_low, head_low)
    g_small[...] = jnp.zeros(g_small.shape, f32)
    for planes in (in_a, in_b, in_g):
        edge = jnp.zeros((images, 4, HALF, C1), bf16)
        planes[:, :, 0] = edge
        planes[:, :, RES + 1] = edge
    for cells in (cells_c, cells_d, cells_g):
        edge = jnp.zeros((images, 3, HALF, cells.shape[-1]), bf16)
        cells[:, :, 0] = edge
        cells[:, :, HALF + 1] = edge

    def load_image(n):
        def step(i, carry):
            sums, squares = carry
            half = i // 2
            v = x_in[half, n, pl.ds((i % 2) * ROWS, ROWS)].astype(f32)
            flat[...] = v.reshape(ROWS * RES, C1)
            for b in range(2):
                w = flat[pl.ds(b, ROWS * HALF, stride=2), :].reshape(ROWS, HALF, C1)
                x_full[n, b, pl.ds(i * ROWS, ROWS)] = w
                sums = sums + fold(w)
                squares = squares + fold(w * w)
            return sums, squares

        sums, squares = lax.fori_loop(0, steps, step, (zero_n, zero_n))
        keep_coefs(coef_n, 0, n, norm_coefs(sums, squares, gain_n(0), gain_n(1), full_pixels))

    each(images, load_image)

    def activate(values, planes, which):
        def image(n):
            scale = row_of(coef_n, which, n, 0)
            offset = row_of(coef_n, which, n, 1)

            def step(i):
                for b in range(2):
                    v = values[n, b, pl.ds(i * ROWS, ROWS)]
                    store_planes(planes, n, b, i * ROWS, silu(v * scale + offset))

            each(steps, step)

        each(images, image)

    def pair_rows(result, n):
        part = result[n * half_pixels : (n + 1) * half_pixels].reshape(HALF, 1, HALF, 2 * C1)
        return jnp.concatenate([part[..., :C1], part[..., C1:]], axis=1).reshape(RES, HALF, C1)

    activate(x_full, in_a, 0)
    for b in range(2):
        out = mm(pair_input(in_a, b, range(4)), pair_fwd[0])
        for n in range(images):
            h1_full[n, b] = pair_rows(out, n)

    def first_hidden(n):
        bias = time_bias[pl.ds(bucket(n), 1), :][:, :C1]

        def step(i, carry):
            sums, squares = carry
            for b in range(2):
                v = h1_full[n, b, pl.ds(i * ROWS, ROWS)] + bias
                h1_full[n, b, pl.ds(i * ROWS, ROWS)] = v
                sums = sums + fold(v)
                squares = squares + fold(v * v)
            return sums, squares

        sums, squares = lax.fori_loop(0, steps, step, (zero_n, zero_n))
        keep_coefs(coef_n, 1, n, norm_coefs(sums, squares, gain_n(2), gain_n(3), full_pixels))

    each(images, first_hidden)
    activate(h1_full, in_b, 1)
    for b in range(2):
        out = mm(pair_input(in_b, b, range(4)), pair_fwd[1])
        for n in range(images):
            xs_full[n, b] = pair_rows(out, n)

    def first_out(n):
        def step(i, carry):
            sums, squares = carry
            for b in range(2):
                v = xs_full[n, b, pl.ds(i * ROWS, ROWS)]
                v = rounded((x_full[n, b, pl.ds(i * ROWS, ROWS)] + v) * root_half)
                xs_full[n, b, pl.ds(i * ROWS, ROWS)] = v
                sums = sums + fold(v)
                squares = squares + fold(v * v)
            return sums, squares

        sums, squares = lax.fori_loop(0, steps, step, (zero_n, zero_n))
        keep_coefs(coef_n, 2, n, norm_coefs(sums, squares, gain_n(4), gain_n(5), full_pixels))

    each(images, first_out)

    def fir_down_image(n):
        scale = row_of(coef_n, 2, n, 0)
        offset = row_of(coef_n, 2, n, 1)
        for b in range(2):
            dy_full[n, b, 0] = jnp.zeros((HALF, C1), f32)
            dy_full[n, b, RES + 1] = jnp.zeros((HALF, C1), f32)

        def act_step(i):
            for b in range(2):
                v = xs_full[n, b, pl.ds(i * ROWS, ROWS)]
                dy_full[n, b, pl.ds(i * ROWS + 1, ROWS)] = silu(v * scale + offset)

        each(steps, act_step)

        def columns(rows):
            even, odd = rows
            return (
                0.125 * (shift_cols(odd, 1) + shift_cols(even, -1)) + 0.375 * (even + odd)
            )

        def taps(ref, b, r0, size):
            return [ref[n, b, pl.ds(r0 + t, size, stride=2)] for t in range(4)]

        def down_step(i):
            size = HALF // 2
            rows = []
            for b in range(2):
                t = taps(dy_full, b, 2 * size * i, size)
                rows.append(0.125 * (t[0] + t[3]) + 0.375 * (t[1] + t[2]))
            store_shifted(cells_c, n, i * size, columns(rows))

        each(2, down_step)
        for b in range(2):
            dy_full[n, b, pl.ds(1, RES)] = xs_full[n, b]

        def skip_step(i):
            size = HALF // 2
            rows = []
            for b in range(2):
                t = taps(dy_full, b, 2 * size * i, size)
                rows.append(0.125 * (t[0] + t[3]) + 0.375 * (t[1] + t[2]))
            fs_low[n, pl.ds(i * size * HALF, size * HALF)] = (
                columns(rows).reshape(size * HALF, C1).astype(bf16)
            )

        each(2, skip_step)

    each(images, fir_down_image)

    def wide_stats(v, which, n, row):
        values = norm_coefs(fold(v), fold(v * v), gain_w(row), gain_w(row + 1), half_pixels)
        keep_coefs(coef_w, which, n, values)
        return values[0][0:1, :], values[1][0:1, :]

    out = mm(cell_input(cells_c, range(3)), down_fwd[...])
    for n in range(images):
        v = out[n * half_pixels : (n + 1) * half_pixels] + time_bias[pl.ds(bucket(n), 1), :][:, C1:]
        h3[n] = v
        scale, offset = wide_stats(v, 0, n, 0)
        store_shifted(cells_d, n, 0, silu(v * scale + offset).reshape(HALF, HALF, HALF_CHANNELS))
    out = mm(cell_input(cells_d, range(3)), wide_fwd[...])
    out = out + mm(fs_low[...].reshape(-1, C1), skip_low[...])
    for n in range(images):
        v = out[n * half_pixels : (n + 1) * half_pixels] * root_half
        x2[n] = v
        scale, offset = wide_stats(v, 1, n, 2)
        n5[n] = (v * scale + offset).astype(bf16)
        qkv[n] = mm(n5[n], attn_low[:, : 3 * HALF_CHANNELS]).astype(bf16)
        q = qkv[n, :, :HALF_CHANNELS]
        k = qkv[n, :, HALF_CHANNELS : 2 * HALF_CHANNELS]
        w = qkv[n, :, 2 * HALF_CHANNELS :]
        logits = mm_nt(q, k) * logit_scale
        powers = jnp.exp(logits - jnp.max(logits, axis=1, keepdims=True))
        weights = powers / jnp.sum(powers, axis=1, keepdims=True)
        probs[n] = weights
        probs_low[n] = weights.astype(bf16)
        att[n] = mm(probs_low[n], w).astype(bf16)
        v = (v + mm(att[n], attn_low[:, 3 * HALF_CHANNELS :])) * root_half
        x3[n] = v
        scale, offset = wide_stats(v, 2, n, 4)
        a6[n] = silu(v * scale + offset).astype(bf16)

    lane = lax.broadcasted_iota(jnp.int32, (RES, 2 * half_pixels), 1)
    source = lax.broadcasted_iota(jnp.int32, (RES, 2 * half_pixels), 0)
    picks = (source == 2 * (lane & (HALF - 1)) + (lane >> 8)).astype(bf16)
    row_lane = (lax.broadcasted_iota(jnp.int32, (HALF, 2 * half_pixels), 1) & (half_pixels - 1)) >> 4
    row_source = lax.broadcasted_iota(jnp.int32, (HALF, 2 * half_pixels), 0)
    component = lax.broadcasted_iota(jnp.int32, (8, half_pixels), 0)

    def spread(halves):
        moved = [mm(half, picks) for half in halves]
        rows = []
        for a in range(2):
            picked = sum(
                jnp.where(2 * row_lane + a == row_source + HALF * h, moved[h], 0.0)
                for h in range(2)
            )
            row = jnp.sum(picked, axis=0, keepdims=True)
            rows.append([row[:, :half_pixels], row[:, half_pixels:]])
        return rows

    loss = jnp.zeros((1, half_pixels), f32)
    head_grad = jnp.zeros((HEAD_ROWS, HALF_CHANNELS), f32)
    for n in range(images):
        moved = mm_nt(head_low[...].astype(bf16), a6[n])
        pred = head_forward(
            [[moved[(dy * 3 + dx) * 8 : (dy * 3 + dx) * 8 + 8] for dx in range(3)] for dy in range(3)]
        )
        wanted = [spread([target[h, n, c] for h in range(2)]) for c in range(3)]
        counted = spread([mask[h, n].astype(f32).astype(bf16) for h in range(2)])
        per_image = 1.0 / counts[pl.ds(bucket(n), 1), :]
        per_image = jnp.concatenate([per_image, per_image], axis=1)
        grad_pred = [[None, None], [None, None]]
        for a in range(2):
            for b in range(2):
                goal = jnp.zeros((8, half_pixels), f32)
                for c in range(3):
                    goal = jnp.where(component == c, wanted[c][a][b], goal)
                error = pred[a][b] - goal
                weight = counted[a][b] * per_image
                loss = loss + weight * jnp.sum(error * error, axis=0, keepdims=True)
                grad_pred[a][b] = rounded(2.0 * error * weight)
        table = head_backward(grad_pred)
        table = jnp.concatenate([table[dy][dx] for dy in range(3) for dx in range(3)], axis=0)
        parts = split_three(table)
        for part in parts:
            head_grad = head_grad + mm(part, a6[n])
        head_rows = head_low[...].astype(bf16)
        grad = sum(mm_tn(part, head_rows) for part in parts)
        v = x3[n]
        values = [coef_w[2, n, kind] for kind in range(4)]
        dy = rounded(grad) * slope(v * values[0][0:1, :] + values[1][0:1, :])
        gain, shift, ca, cb, cd = norm_grad_coefs(
            fold(dy), fold(dy * v), gain_w(4), values[2], values[3], half_pixels
        )
        g_small[WIDE_NORM_ROW + 4 : WIDE_NORM_ROW + 5, :] += gain[0:1, :]
        g_small[WIDE_NORM_ROW + 5 : WIDE_NORM_ROW + 6, :] += shift[0:1, :]
        grad_third = dy * ca[0:1, :] + v * cb[0:1, :] + cd[0:1, :]
        dwide[n] = grad_third
    g_small[0:HEAD_ROWS, :] = head_grad
    g_small[LOSS_ROW : LOSS_ROW + 1, :] = jnp.broadcast_to(
        jnp.sum(loss, axis=1, keepdims=True), (1, HALF_CHANNELS)
    )

    for n in range(images):
        grad_attn = (dwide[n] * root_half).astype(bf16)
        dout[n] = grad_attn
        grad_att = mm_nt(grad_attn, attn_low[:, 3 * HALF_CHANNELS :]).astype(bf16)
        q = qkv[n, :, :HALF_CHANNELS]
        k = qkv[n, :, HALF_CHANNELS : 2 * HALF_CHANNELS]
        w = qkv[n, :, 2 * HALF_CHANNELS :]
        grad_probs = mm_nt(grad_att, w)
        weights = probs[n]
        inner = jnp.sum(weights * grad_probs, axis=1, keepdims=True)
        grad_scores = (weights * (grad_probs - inner)).astype(bf16)
        dqkv[n, :, :HALF_CHANNELS] = (mm(grad_scores, k) * logit_scale).astype(bf16)
        dqkv[n, :, HALF_CHANNELS : 2 * HALF_CHANNELS] = (mm_tn(grad_scores, q) * logit_scale).astype(bf16)
        dqkv[n, :, 2 * HALF_CHANNELS :] = mm_tn(probs_low[n], grad_att).astype(bf16)
    keep_columns(
        g_attn, 0, mm_tn(n5[...].reshape(-1, HALF_CHANNELS), dqkv[...].reshape(-1, 3 * HALF_CHANNELS))
    )
    keep_columns(
        g_attn,
        6 * HALF_CHANNELS,
        mm_tn(att[...].reshape(-1, HALF_CHANNELS), dout[...].reshape(-1, HALF_CHANNELS)),
    )
    for n in range(images):
        dy = mm_nt(dqkv[n], attn_low[:, : 3 * HALF_CHANNELS])
        v = x2[n]
        gain, shift, ca, cb, cd = norm_grad_coefs(
            fold(dy), fold(dy * v), gain_w(2), coef_w[1, n, 2], coef_w[1, n, 3], half_pixels
        )
        g_small[WIDE_NORM_ROW + 2 : WIDE_NORM_ROW + 3, :] += gain[0:1, :]
        g_small[WIDE_NORM_ROW + 3 : WIDE_NORM_ROW + 4, :] += shift[0:1, :]
        grad = dy * ca[0:1, :] + v * cb[0:1, :] + cd[0:1, :] + dwide[n] * root_half
        store_shifted(cells_g, n, 0, (grad * root_half).reshape(HALF, HALF, HALF_CHANNELS))

    center = cells_g[:, 1, 1 : HALF + 1].reshape(-1, HALF_CHANNELS)
    for dy in range(3):
        product = mm_tn(cell_input(cells_d, [dy]), center)
        for k in range(3):
            keep_columns(
                g_wide,
                (dy * 3 + k) * 2 * HALF_CHANNELS,
                product[k * HALF_CHANNELS : (k + 1) * HALF_CHANNELS],
            )
    keep_columns(g_down, SKIP_ROW, mm_tn(fs_low[...].reshape(-1, C1), center))
    dfs[...] = mm_nt(center, skip_low[...]).reshape(dfs.shape)
    out = mm_nt(cell_input(cells_g, range(3)), wide_bwd[...])
    bucket_rows = lax.broadcasted_iota(jnp.int32, (NB, HALF_CHANNELS), 0)
    time_wide = jnp.zeros((NB, HALF_CHANNELS), f32)
    for n in range(images):
        v = h3[n]
        dy = out[n * half_pixels : (n + 1) * half_pixels] * slope(
            v * row_of(coef_w, 0, n, 0) + row_of(coef_w, 0, n, 1)
        )
        gain, shift, ca, cb, cd = norm_grad_coefs(
            fold(dy), fold(dy * v), gain_w(0), coef_w[0, n, 2], coef_w[0, n, 3], half_pixels
        )
        g_small[WIDE_NORM_ROW : WIDE_NORM_ROW + 1, :] += gain[0:1, :]
        g_small[WIDE_NORM_ROW + 1 : WIDE_NORM_ROW + 2, :] += shift[0:1, :]
        grad = dy * ca[0:1, :] + v * cb[0:1, :] + cd[0:1, :]
        time_wide = time_wide + jnp.where(bucket_rows == bucket(n), total(fold(grad)), 0.0)
        store_shifted(cells_g, n, 0, grad.reshape(HALF, HALF, HALF_CHANNELS))
    g_small[TIME_WIDE_ROW : TIME_WIDE_ROW + NB, :] = time_wide

    center = cells_g[:, 1, 1 : HALF + 1].reshape(-1, HALF_CHANNELS)
    for dy in range(3):
        product = mm_tn(cell_input(cells_c, [dy]), center)
        for k in range(3):
            keep_columns(g_down, (dy * 3 + k) * 2 * C1, product[k * C1 : (k + 1) * C1])
    dnarrow[...] = mm_nt(cell_input(cells_g, range(3)), down_bwd[...]).reshape(dnarrow.shape)

    def up_parts(ref, n, i, size):
        here = pl.ds(i * size * HALF, size * HALF)
        g = ref[n, here].reshape(size, HALF, C1)
        lane_rows = lax.broadcasted_iota(jnp.int32, g.shape, 0) + i * size
        above = ref[n, pl.ds(jnp.maximum(i * size - 1, 0) * HALF, HALF)].reshape(1, HALF, C1)
        below = ref[n, pl.ds(jnp.minimum((i + 1) * size, HALF - 1) * HALF, HALF)].reshape(1, HALF, C1)
        above = jnp.where(lane_rows == 0, 0.0, jnp.concatenate([above, g[:-1]], axis=0))
        below = jnp.where(lane_rows == HALF - 1, 0.0, jnp.concatenate([g[1:], below], axis=0))
        result = []
        for rows in (0.375 * g + 0.125 * above, 0.375 * g + 0.125 * below):
            result.append(
                (
                    0.375 * rows + 0.125 * shift_cols(rows, 1),
                    0.375 * rows + 0.125 * shift_cols(rows, -1),
                )
            )
        return result

    def third_norm(n):
        size = HALF // 4
        scale = row_of(coef_n, 2, n, 0)
        offset = row_of(coef_n, 2, n, 1)

        def step(i, carry):
            sum_dy, sum_dyv = carry
            parts = up_parts(dnarrow, n, i, size)
            for b in range(2):
                g = jnp.stack([parts[0][b], parts[1][b]], axis=1).reshape(2 * size, HALF, C1)
                v = xs_full[n, b, pl.ds(i * 2 * size, 2 * size)]
                dy = g * slope(v * scale + offset)
                dy_full[n, b, pl.ds(i * 2 * size, 2 * size)] = dy
                sum_dy = sum_dy + fold(dy)
                sum_dyv = sum_dyv + fold(dy * v)
            return sum_dy, sum_dyv

        sum_dy, sum_dyv = lax.fori_loop(0, 4, step, (zero_n, zero_n))
        gain, shift, ca, cb, cd = norm_grad_coefs(
            sum_dy, sum_dyv, gain_n(4), coef_n[2, n, 2], coef_n[2, n, 3], full_pixels
        )
        g_small[NARROW_NORM_ROW + 4 : NARROW_NORM_ROW + 5, :C1] += gain[0:1, :]
        g_small[NARROW_NORM_ROW + 5 : NARROW_NORM_ROW + 6, :C1] += shift[0:1, :]

        def finish(i):
            parts = up_parts(dfs, n, i, size)
            for b in range(2):
                g = jnp.stack([parts[0][b], parts[1][b]], axis=1).reshape(2 * size, HALF, C1)
                here = pl.ds(i * 2 * size, 2 * size)
                v = xs_full[n, b, here]
                g = g + dy_full[n, b, here] * ca[0:1, :] + v * cb[0:1, :] + cd[0:1, :]
                store_planes(in_g, n, b, i * 2 * size, rounded(g) * root_half)

        each(4, finish)

    each(images, third_norm)

    def pair_gradient(planes, member):
        products = None
        for b in range(2):
            grads = jnp.concatenate([plane_block(in_g, EVEN + b, a + 1) for a in range(2)], axis=1)
            part = [mm_tn(grads, pair_input(planes, b, jjs)) for jjs in ((0, 1), (2, 3))]
            products = part if products is None else [p + q for p, q in zip(products, part)]
        for dy in range(3):
            blocks = []
            for a in range(2):
                jj = dy + a
                wide_part = products[jj // 2][a * C1 : (a + 1) * C1]
                blocks.append(wide_part[:, (jj % 2) * 3 * C1 : (jj % 2 + 1) * 3 * C1])
            both = blocks[0] + blocks[1]
            for k in range(3):
                row = (member * 9 + dy * 3 + k) * C1
                g_pair[row : row + C1, :] = both[:, k * C1 : (k + 1) * C1].T

    def back_through(member, values, which, gain_row, last):
        for b in range(2):
            out = mm_nt(pair_input(in_g, b, range(4)), pair_bwd[member])
            for n in range(images):
                dy_full[n, b, pl.ds(0, RES)] = pair_rows(out, n)
        bucket_rows = lax.broadcasted_iota(jnp.int32, (NB, C1), 0)

        def image(n):
            scale = row_of(coef_n, which, n, 0)
            offset = row_of(coef_n, which, n, 1)

            def step(i, carry):
                sum_dy, sum_dyv = carry
                here = pl.ds(i * ROWS, ROWS)
                for b in range(2):
                    v = values[n, b, here]
                    dy = dy_full[n, b, here] * slope(v * scale + offset)
                    if not last:
                        dy_full[n, b, here] = dy
                    sum_dy = sum_dy + fold(dy)
                    sum_dyv = sum_dyv + fold(dy * v)
                return sum_dy, sum_dyv

            sum_dy, sum_dyv = lax.fori_loop(0, steps, step, (zero_n, zero_n))
            gain, shift, ca, cb, cd = norm_grad_coefs(
                sum_dy, sum_dyv, gain_n(gain_row), coef_n[which, n, 2], coef_n[which, n, 3], full_pixels
            )
            row = NARROW_NORM_ROW + gain_row
            g_small[row : row + 1, :C1] += gain[0:1, :]
            g_small[row + 1 : row + 2, :C1] += shift[0:1, :]
            if last:
                return

            def finish(i, carry):
                here = pl.ds(i * ROWS, ROWS)
                for b in range(2):
                    v = values[n, b, here]
                    g = dy_full[n, b, here] * ca[0:1, :] + v * cb[0:1, :] + cd[0:1, :]
                    carry = carry + fold(g)
                    store_planes(in_g, n, b, i * ROWS, g)
                return carry

            sums = total(lax.fori_loop(0, steps, finish, zero_n))
            g_small[TIME_NARROW_ROW : TIME_NARROW_ROW + NB, :C1] += jnp.where(
                bucket_rows == bucket(n), sums, 0.0
            )

        each(images, image)

    pair_gradient(in_b, 1)
    back_through(1, h1_full, 1, 2, False)
    pair_gradient(in_a, 0)
    back_through(0, x_full, 0, 0, True)


def main_call(images, *operands):
    n = images
    vm = pltpu.VMEM
    full = (n, 2, RES, HALF, C1)
    planes = (n, 4, RES + 2, HALF, C1)
    wide = HALF_CHANNELS
    square = (n, HALF * HALF, wide)
    scratch = [
        vm((2, 12 * C1, 2 * C1), bf16),
        vm((2, 2 * C1, 12 * C1), bf16),
        vm((9 * C1, wide), bf16),
        vm((C1, 9 * wide), bf16),
        vm((9 * wide, wide), bf16),
        vm((wide, 9 * wide), bf16),
        vm((C1, wide), bf16),
        vm((wide, 4 * wide), bf16),
        vm((HEAD_ROWS, wide), f32),
        vm(full, f32),
        vm(full, f32),
        vm(full, f32),
        vm((n, 2, RES + 2, HALF, C1), f32),
        vm(planes, bf16),
        vm(planes, bf16),
        vm(planes, bf16),
        vm((ROWS * RES, C1), f32),
        vm((n, 3, HALF + 2, HALF, C1), bf16),
        vm((n, 3, HALF + 2, HALF, wide), bf16),
        vm((n, 3, HALF + 2, HALF, wide), bf16),
        vm((n, HALF * HALF, C1), bf16),
        vm((n, HALF * HALF, C1), f32),
        vm(square, f32),
        vm(square, f32),
        vm(square, f32),
        vm(square, bf16),
        vm((n, HALF * HALF, 3 * wide), bf16),
        vm(square, f32),
        vm(square, bf16),
        vm(square, bf16),
        vm(square, bf16),
        vm(square, f32),
        vm(square, bf16),
        vm((n, HALF * HALF, 3 * wide), bf16),
        vm((n, HALF * HALF, C1), f32),
        vm((3, n, 4, 8, C1), f32),
        vm((3, n, 4, 8, wide), f32),
    ]
    whole = pl.BlockSpec(memory_space=pltpu.VMEM)
    return pl.pallas_call(
        main_kernel,
        out_shape=[
            jax.ShapeDtypeStruct(shape, f32)
            for shape in PIECES
        ],
        in_specs=[pl.BlockSpec(memory_space=pltpu.SMEM)] + [whole] * 13,
        out_specs=[whole] * 5,
        scratch_shapes=scratch,
        compiler_params=pltpu.CompilerParams(vmem_limit_bytes=VMEM_LIMIT),
        cost_estimate=pl.CostEstimate(flops=8 * 10**9, bytes_accessed=12 * 10**6, transcendentals=0),
    )(*operands)


def partners(dp_size):
    dp = lax.axis_index("dp")
    sp = lax.axis_index("sp")

    def flip(k):
        unit = 1 << k
        side = (dp // unit) % 2
        return side, (dp + unit * (1 - 2 * side), sp)

    core, near = flip(0), flip(1)
    second = core[0]

    def pick(first, other):
        return first + second * (other - first)

    stages = [
        core,
        (pick(near[0], sp), (pick(near[1][0], dp), pick(sp, 1 - sp))),
        (pick(sp, near[0]), (pick(dp, near[1][0]), pick(1 - sp, sp))),
    ]
    for k in range(2, (dp_size - 1).bit_length()):
        stages.append(flip(k))
    return stages


def greet(stages):
    barrier = pltpu.get_barrier_semaphore()
    for _, other in stages:
        pl.semaphore_signal(barrier, inc=1, device_id=other, device_id_type=MESH)
    pl.semaphore_wait(barrier, len(stages))


def send(source, target, sems, index, other):
    return pltpu.make_async_remote_copy(
        src_ref=source,
        dst_ref=target,
        send_sem=sems.at[0, index],
        recv_sem=sems.at[1, index],
        device_id=other,
        device_id_type=MESH,
    )


def images_kernel(
    dp_size, buckets, features, target, mask, mask_in, x_out, target_out, mask_out, counts_out,
    totals, arrived, sems, local_sems, count_sems,
):
    stages = partners(dp_size)
    dp = lax.axis_index("dp")
    sp = lax.axis_index("sp")
    greet(stages)
    copies = [
        send(source.at[1 - sp], out.at[sp], sems, i, (dp, 1 - sp))
        for i, (source, out) in enumerate(((features, x_out), (target, target_out), (mask, mask_out)))
    ]
    for copy in copies:
        copy.start()
    keeps = [
        pltpu.make_async_copy(source.at[sp], out.at[sp], local_sems.at[i])
        for i, (source, out) in enumerate(((features, x_out), (target, target_out), (mask, mask_out)))
    ]
    for copy in keeps:
        copy.start()
    rows = lax.broadcasted_iota(jnp.int32, (NB, 128), 0)
    counted = jnp.zeros((NB, 128), f32)
    images = mask_in.shape[1]
    for i in range(2 * images):
        pixels = mask_in[i // images, i % images].astype(f32)
        number = jnp.sum(jnp.sum(pixels, axis=0, keepdims=True), axis=1, keepdims=True)
        counted = counted + jnp.where(rows == buckets[i], number, 0.0)
    totals[0] = counted
    for s, (_, other) in enumerate(stages):
        copy = send(totals.at[s], arrived.at[s], count_sems, s, other)
        copy.start()
        copy.wait()
        totals[s + 1] = totals[s] + arrived[s]
    counts_out[...] = totals[len(stages)]
    for copy in keeps + copies:
        copy.wait()


def images_call(dp_size, buckets, features, target, mask):
    stages = (dp_size - 1).bit_length() + 1
    anywhere = pl.BlockSpec(memory_space=pl.ANY)
    whole = pl.BlockSpec(memory_space=pltpu.VMEM)
    shapes = [jax.ShapeDtypeStruct(v.shape, v.dtype) for v in (features, target, mask)]
    return pl.pallas_call(
        functools.partial(images_kernel, dp_size),
        out_shape=shapes + [jax.ShapeDtypeStruct((NB, 128), f32)],
        in_specs=[pl.BlockSpec(memory_space=pltpu.SMEM)] + [anywhere] * 3 + [whole],
        out_specs=[anywhere] * 3 + [whole],
        scratch_shapes=[
            pltpu.VMEM((stages + 1, NB, 128), f32),
            pltpu.VMEM((stages, NB, 128), f32),
            pltpu.SemaphoreType.DMA((2, 3)),
            pltpu.SemaphoreType.DMA((3,)),
            pltpu.SemaphoreType.DMA((2, stages)),
        ],
        compiler_params=pltpu.CompilerParams(collective_id=0, has_side_effects=True),
    )(buckets, features, target, mask, mask)


def chunk_of(rows):
    return next(c for c in (128, 96, 72, 64, 48, 40, 32, 24, 16, 8) if rows % c == 0)


def add_rows(target, base, source, offset, rows):
    size = chunk_of(rows)

    def step(i):
        here = pl.ds(pl.multiple_of(base + i * size, 8), size)
        target[here, :] = target[here, :] + source[pl.ds(pl.multiple_of(offset + i * size, 8), size), :]

    each(rows // size, step)


class Piece:
    def __init__(self, source, arrived, out, sems, stages):
        self.source, self.arrived, self.out, self.sems, self.stages = source, arrived, out, sems, stages
        rows = source.shape[0]
        self.plan = []
        base = 0
        lowest = 0
        for side, other in stages:
            halved = rows % 16 == 0
            rows = rows // 2 if halved else rows
            self.plan.append((side, other, halved, rows, base, lowest))
            lowest = lowest + side * rows if halved else lowest
            base += rows
        self.rows, self.lowest = rows, lowest
        self.copies = {}

    def region(self, s, side):
        halved, rows = self.plan[s][2:4]
        if s == 0:
            ref, base = self.source, 0
        else:
            ref, base = self.arrived, self.plan[s - 1][4]
        return ref, (base + side * rows if halved else base)

    def scatter_start(self, s):
        side, other, halved, rows, base, _ = self.plan[s]
        ref, first = self.region(s, 1 - side)
        copy = send(
            ref.at[pl.ds(pl.multiple_of(first, 8), rows)],
            self.arrived.at[pl.ds(base, rows)],
            self.sems,
            s,
            other,
        )
        copy.start()
        self.copies[s] = copy

    def scatter_end(self, s):
        side, other, halved, rows, base, _ = self.plan[s]
        self.copies[s].wait()
        ref, first = self.region(s, side)
        add_rows(self.arrived, base, ref, first, rows)
        if s + 1 == len(self.stages):
            self.out[pl.ds(pl.multiple_of(self.lowest, 8), rows), :] = self.arrived[base : base + rows, :]

    def gather_start(self, s):
        side, other, halved, rows, base, lowest = self.plan[s]
        if halved:
            here = pl.ds(pl.multiple_of(lowest + side * rows, 8), rows)
            copy = send(self.out.at[here], self.out.at[here], self.sems, len(self.stages) + s, other)
            copy.start()
            self.copies[len(self.stages) + s] = copy

    def gather_end(self, s):
        if self.plan[s][2]:
            self.copies[len(self.stages) + s].wait()

    def step(self, t):
        count = len(self.stages)
        if 0 < t <= count:
            self.scatter_end(t - 1)
        elif t > count:
            self.gather_end(2 * count - t)
        if t < count:
            self.scatter_start(t)
        elif t < 2 * count:
            self.gather_start(2 * count - 1 - t)


def arrived_rows(rows, stages):
    needed = 0
    for _ in range(stages):
        rows = rows // 2 if rows % 16 == 0 else rows
        needed += rows
    return needed


def sum_kernel(dp_size, *refs):
    count = len(PIECES)
    sources, outs, arrived, sems = (refs[i * count : (i + 1) * count] for i in range(4))
    stages = partners(dp_size)
    greet(stages)
    pieces = [Piece(*parts, stages) for parts in zip(sources, arrived, outs, sems)]
    last = 2 * len(stages)
    for t in range(last + count):
        for i, piece in enumerate(pieces):
            if 0 <= t - i <= last:
                piece.step(t - i)


def sum_call(dp_size, partial):
    stages = (dp_size - 1).bit_length() + 1
    whole = pl.BlockSpec(memory_space=pltpu.VMEM)
    return pl.pallas_call(
        functools.partial(sum_kernel, dp_size),
        out_shape=[jax.ShapeDtypeStruct(shape, f32) for shape in PIECES],
        in_specs=[whole] * len(PIECES),
        out_specs=[whole] * len(PIECES),
        scratch_shapes=[pltpu.VMEM((arrived_rows(rows, stages), lanes), f32) for rows, lanes in PIECES]
        + [pltpu.SemaphoreType.DMA((2, 2 * stages)) for _ in PIECES],
        compiler_params=pltpu.CompilerParams(
            collective_id=1, has_side_effects=True, vmem_limit_bytes=VMEM_LIMIT
        ),
    )(*partial)


def adamw(weight, grad, first, second, rate):
    first = beta_one * first + (1.0 - beta_one) * grad
    second = beta_two * second + (1.0 - beta_two) * grad * grad
    scale = rate / (1.0 - beta_one**STEP)
    root = jnp.sqrt(second * (1.0 / (1.0 - beta_two**STEP))) + adam_epsilon
    return weight * (1.0 - rate * decay_rate) - scale * first / root, first, second


def update_kernel(*refs):
    g_attn, g_wide, g_down, g_pair, g_small = refs[:5]
    members = [refs[5 + 3 * i : 8 + 3 * i] for i in range(9)]
    outs = [refs[32 + 3 * i : 35 + 3 * i] for i in range(9)]
    loss_out = refs[59]

    def blocks(member, grad, block_rows, base, count):
        size = 64

        def step(i):
            block = i // (block_rows // size)
            row = (i % (block_rows // size)) * size
            here = pl.ds(pl.multiple_of(block * block_rows + row, 8), size)
            columns = members[member][0].shape[1] // 128
            for c in range(columns):
                lanes = slice(c * 128, (c + 1) * 128)
                g = grad[pl.ds(pl.multiple_of(base + (block * columns + c) * block_rows + row, 8), size), :]
                w, m, v = (ref[here, lanes] for ref in members[member])
                for out, value in zip(outs[member], adamw(w, g, m, v, rate_matrix)):
                    out[here, lanes] = value

        each(count * block_rows // size, step)

    def single(member, index, grad, rate):
        w, m, v = (ref[index] for ref in members[member])
        for out, value in zip(outs[member], adamw(w, grad, m, v, rate)):
            out[index] = value

    blocks(0, g_pair, C1, 0, 18)
    blocks(1, g_down, C1, 0, 9)
    blocks(2, g_wide, HALF_CHANNELS, 0, 9)
    blocks(3, g_down, C1, SKIP_ROW, 1)
    blocks(4, g_attn, HALF_CHANNELS, 0, 1)
    for tap in range(9):
        single(5, (tap,), g_small[tap * 8 : tap * 8 + 3, :], rate_matrix)
    single(6, (slice(None), slice(None)), g_small[NARROW_NORM_ROW : NARROW_NORM_ROW + 6, :C1], rate_vector)
    single(7, (slice(None), slice(None)), g_small[WIDE_NORM_ROW : WIDE_NORM_ROW + 6, :], rate_vector)
    single(
        8, (slice(None), slice(0, C1)), g_small[TIME_NARROW_ROW : TIME_NARROW_ROW + NB, :C1], rate_vector
    )
    single(
        8, (slice(None), slice(C1, None)), g_small[TIME_WIDE_ROW : TIME_WIDE_ROW + NB, :], rate_vector
    )
    loss_out[...] = g_small[LOSS_ROW : LOSS_ROW + 1, :128]


def update_call(grads, members):
    whole = pl.BlockSpec(memory_space=pltpu.VMEM)
    flat = [v for member in members for v in member]
    return pl.pallas_call(
        update_kernel,
        out_shape=[jax.ShapeDtypeStruct(v.shape, f32) for v in flat]
        + [jax.ShapeDtypeStruct((1, 128), f32)],
        in_specs=[whole] * (5 + len(flat)),
        out_specs=[whole] * (len(flat) + 1),
        compiler_params=pltpu.CompilerParams(vmem_limit_bytes=VMEM_LIMIT),
    )(*grads, *flat)


def on_device(
    features,
    target,
    pixel_mask,
    buckets,
    conv_pair,
    down_conv,
    conv_wide,
    skip_proj,
    attn_proj,
    head_conv,
    norm_narrow,
    norm_wide,
    time_bias,
    conv_pair_mom,
    down_conv_mom,
    conv_wide_mom,
    skip_proj_mom,
    attn_proj_mom,
    head_conv_mom,
    norm_narrow_mom,
    norm_wide_mom,
    time_bias_mom,
    conv_pair_sq,
    down_conv_sq,
    conv_wide_sq,
    skip_proj_sq,
    attn_proj_sq,
    head_conv_sq,
    norm_narrow_sq,
    norm_wide_sq,
    time_bias_sq,
):
    dp_size = lax.axis_size("dp")
    images = features.shape[0] // 2

    def halves(tensor):
        return tensor.reshape((2, images) + tensor.shape[1:])

    def flat(tensor):
        return tensor.reshape(-1, tensor.shape[-1])

    def head_rows(tensor):
        return jnp.transpose(tensor, (0, 1, 3, 2)).reshape(9, 3, HALF_CHANNELS)

    images_in = images_call(
        dp_size,
        buckets,
        halves(features),
        halves(jnp.transpose(target, (0, 3, 1, 2))),
        halves(pixel_mask),
    )
    params = (
        flat(conv_pair),
        flat(down_conv),
        flat(conv_wide),
        skip_proj,
        attn_proj,
        head_rows(head_conv),
        norm_narrow,
        norm_wide,
        time_bias,
    )
    firsts = (
        flat(conv_pair_mom),
        flat(down_conv_mom),
        flat(conv_wide_mom),
        skip_proj_mom,
        attn_proj_mom,
        head_rows(head_conv_mom),
        norm_narrow_mom,
        norm_wide_mom,
        time_bias_mom,
    )
    seconds = (
        flat(conv_pair_sq),
        flat(down_conv_sq),
        flat(conv_wide_sq),
        skip_proj_sq,
        attn_proj_sq,
        head_rows(head_conv_sq),
        norm_narrow_sq,
        norm_wide_sq,
        time_bias_sq,
    )
    partial = main_call(images, buckets, *images_in, *params)
    summed = sum_call(dp_size, partial)
    results = update_call(summed, list(zip(params, firsts, seconds)))
    shaped = []
    for member, like in enumerate((conv_pair, down_conv, conv_wide, skip_proj, attn_proj)):
        shaped.extend(v.reshape(like.shape) for v in results[3 * member : 3 * member + 3])
    for v in results[15:18]:
        shaped.append(jnp.transpose(v.reshape(3, 3, 3, HALF_CHANNELS), (0, 1, 3, 2)))
    shaped.extend(results[18:27])
    return (results[27][0, 0], images_in[3][:, 0]) + tuple(shaped)


def solution(mesh):
    placed = (
        P("dp", "sp", None, None),
        P("dp", "sp", None, None),
        P("dp", "sp", None),
        P("dp"),
        P(),
        P(),
        P(),
        P(),
        P(),
        P(),
        P(),
        P(),
        P(),
        P(),
        P(),
        P(),
        P(),
        P(),
        P(),
        P(),
        P(),
        P(),
        P(),
        P(),
        P(),
        P(),
        P(),
        P(),
        P(),
        P(),
        P(),
    )
    return jax.shard_map(
        on_device,
        mesh=mesh,
        in_specs=placed,
        out_specs=(
            P(),
            P(),
            P(),
            P(),
            P(),
            P(),
            P(),
            P(),
            P(),
            P(),
            P(),
            P(),
            P(),
            P(),
            P(),
            P(),
            P(),
            P(),
            P(),
            P(),
            P(),
            P(),
            P(),
            P(),
            P(),
            P(),
            P(),
            P(),
            P(),
        ),
        check_vma=False,
    )
```

profile of v0, /device:TPU:0, one launch (start us, length us, event | category | flops | bytes accessed | tf_op | source)
XLA Modules:
  0.0 158.3 jit_solution(4549577916254984404)
XLA Ops:
  0.7 20.7 %shard_map.518 = (bf16[2,2,16,32,128]{4,3,2,1,0:T(8,128)(2,1)}, bf16[2,2,3,16,32]{4,3,2,1,0:T(8,128)(2,1)}, s32[2,2,16,32]{3,2,1,0:T(8,128)}, f32[8,128]{1,0:T(8,128)}) custom-call(s32[4]{0:T(128)} %buckets.3, bf16[2,2,16,32,128]{4,3,2,1,0:T(8,128)(2,1)} %bitcast.55, bf16[2,2,3,16,32]{4,3,2,1,0:T(8,128)(2,1)} %bitcast.58, s32[2,2,16,32]{3,2,1,0:T(8,128)} %bitcast.56, ...), custom_call_target="tpu_custom_call" | custom-call | tf_op jit(solution)/shard_map/pallas_call | solution.py:879
  21.4 1.3 slice_reduce_fusion
  22.7 31.8 %shard_map.519 = (f32[2048,128]{1,0:T(8,128)}, f32[4608,128]{1,0:T(8,128)}, f32[2560,128]{1,0:T(8,128)}, f32[2304,128]{1,0:T(8,128)}, f32[128,256]{1,0:T(8,128)}) custom-call(s32[4]{0:T(128)} %buckets.3, bf16[2,2,16,32,128]{4,3,2,1,0:T(8,128)(2,1)} %get-tuple-element.71.x_in, bf16[2,2,3,16,32]{4,3,2,1,0:T(8,128)(2,1)} %get-tuple-element.72.target, ...), custom_call_target="tpu_custom_call" | custom-call | flops 8000000000 | bytes 12000000 | tf_op jit(solution)/shard_map/pallas_call | solution.py:779
  54.5 83.7 %shard_map.520 = (f32[2048,128]{1,0:T(8,128)}, f32[4608,128]{1,0:T(8,128)}, f32[2560,128]{1,0:T(8,128)}, f32[2304,128]{1,0:T(8,128)}, f32[128,256]{1,0:T(8,128)}) custom-call(f32[2048,128]{1,0:T(8,128)} %get-tuple-element.75.refs_0_, f32[4608,128]{1,0:T(8,128)} %get-tuple-element.76.refs_1_, f32[2560,128]{1,0:T(8,128)} %get-tuple-element.77.refs_2_, ...), custom_call_target="tpu_custom_call" | custom-call | tf_op jit(solution)/shard_map/pallas_call | solution.py:1002
  138.2 20.0 %shard_map.521 = (f32[2304,128]{1,0:T(8,128)}, f32[2304,128]{1,0:T(8,128)}, f32[2304,128]{1,0:T(8,128)}, f32[1152,256]{1,0:T(8,128)}, f32[1152,256]{1,0:T(8,128)...) custom-call(f32[2048,128]{1,0:T(8,128)} %get-tuple-element.80.refs_0, ...), custom_call_target="tpu_custom_call" | custom-call | tf_op jit(solution)/shard_map/pallas_call | solution.py:1072
where the time goes:
time: 159 us; the launch traced here: 158 us
  Pallas kernels  156 us (98%)
    pallas_call x1, Pallas kernels, sum_call(): pl.pallas_call(functools.partial(sum_kernel, dp_size), out_shape=[jax.Sha...  83.7 us
    pallas_call x1, Pallas kernels, main_call(): pl.pallas_call(main_kernel, out_shape=[jax.ShapeDtypeStruct(shape, f32) f...  31.8 us
    pallas_call x1, Pallas kernels, images_call(): pl.pallas_call(functools.partial(images_kernel, dp_size), out_shape=shape...  20.7 us
    pallas_call x1, Pallas kernels, update_call(): pl.pallas_call(update_kernel, out_shape=[jax.ShapeDtypeStruct(v.shape, f3...  20 us

commit v1 on v0

--- a/solution.py
+++ b/solution.py
@@ -267,13 +267,48 @@
 
 
 def main_kernel(
-    buckets, x_in, target, mask, counts, pair, down, wide, skip, attn, head, gains_narrow, gains_wide, time_bias,
-    g_attn, g_wide, g_down, g_pair, g_small,
+    dp_size,
+    buckets, features, target_rows, mask_rows, mask_local, pair_all, down_all, wide_all, skip_all, attn_all, head_all,
+    gains_narrow, gains_wide, time_bias,
+    sum_attn, sum_wide, sum_down, sum_pair, sum_small, counts,
+    x_in, target, mask, pair, down, wide, skip, attn, head, g_attn, g_wide, g_down, g_pair, g_small,
+    arrived_attn, arrived_wide, arrived_down, arrived_pair, arrived_small,
+    sems_attn, sems_wide, sems_down, sems_pair, sems_small,
+    totals, arrived_totals, image_sems, local_sems, count_sems, weight_sems,
     pair_fwd, pair_bwd, down_fwd, down_bwd, wide_fwd, wide_bwd, skip_low, attn_low, head_low,
     x_full, h1_full, xs_full, dy_full, in_a, in_b, in_g, flat,
     cells_c, cells_d, cells_g, fs_low, dfs, h3, x2, x3, n5, qkv, probs, probs_low, att, a6, dwide, dout, dqkv, dnarrow,
     coef_n, coef_w,
 ):
+    loads = [
+        pltpu.make_async_copy(source, ref, weight_sems.at[i])
+        for i, (source, ref) in enumerate(
+            (
+                (pair_all, pair),
+                (down_all, down),
+                (wide_all, wide),
+                (skip_all, skip),
+                (attn_all, attn),
+                (head_all, head),
+            )
+        )
+    ]
+    stages = partners(dp_size)
+    greet(stages)
+    here = (lax.axis_index("dp"), 1 - lax.axis_index("sp"))
+    moved = ((features, x_in), (target_rows, target), (mask_rows, mask))
+    side = lax.axis_index("sp")
+    arrivals = [
+        send(source.at[1 - side], out.at[side], image_sems, i, here) for i, (source, out) in enumerate(moved)
+    ]
+    for copy in arrivals:
+        copy.start()
+    keeps = [
+        pltpu.make_async_copy(source.at[side], out.at[side], local_sems.at[i])
+        for i, (source, out) in enumerate(moved)
+    ]
+    for copy in keeps + loads:
+        copy.start()
     images = x_in.shape[1]
     position = lax.axis_index("sp")
     steps = RES // ROWS
@@ -298,6 +333,10 @@
     def row_of(ref, which, n, kind):
         return ref[which, n, kind, 0:1, :]
 
+    counting = Counting(buckets, mask_local, totals, arrived_totals, count_sems, stages)
+    counting.step()
+    for copy in loads:
+        copy.wait()
     prepare_weights(pair, down, wide, skip, attn, head, pair_fwd, pair_bwd, down_fwd, down_bwd, wide_fwd, wide_bwd, skip_low, attn_low, head_low)
     g_small[...] = jnp.zeros(g_small.shape, f32)
     for planes in (in_a, in_b, in_g):
@@ -308,6 +347,10 @@
         edge = jnp.zeros((images, 3, HALF, cells.shape[-1]), bf16)
         cells[:, :, 0] = edge
         cells[:, :, HALF + 1] = edge
+
+    for copy in keeps + arrivals:
+        copy.wait()
+    counting.step()
 
     def load_image(n):
         def step(i, carry):
@@ -346,6 +389,7 @@
         return jnp.concatenate([part[..., :C1], part[..., C1:]], axis=1).reshape(RES, HALF, C1)
 
     activate(x_full, in_a, 0)
+    counting.step()
     for b in range(2):
         out = mm(pair_input(in_a, b, range(4)), pair_fwd[0])
         for n in range(images):
@@ -368,6 +412,7 @@
 
     each(images, first_hidden)
     activate(h1_full, in_b, 1)
+    counting.step()
     for b in range(2):
         out = mm(pair_input(in_b, b, range(4)), pair_fwd[1])
         for n in range(images):
@@ -388,6 +433,8 @@
         keep_coefs(coef_n, 2, n, norm_coefs(sums, squares, gain_n(4), gain_n(5), full_pixels))
 
     each(images, first_out)
+
+    counting.step()
 
     def fir_down_image(n):
         scale = row_of(coef_n, 2, n, 0)
@@ -470,6 +517,8 @@
         x3[n] = v
         scale, offset = wide_stats(v, 2, n, 4)
         a6[n] = silu(v * scale + offset).astype(bf16)
+
+    counting.finish(counts)
 
     lane = lax.broadcasted_iota(jnp.int32, (RES, 2 * half_pixels), 1)
     source = lax.broadcasted_iota(jnp.int32, (RES, 2 * half_pixels), 0)
@@ -727,16 +776,37 @@
     back_through(1, h1_full, 1, 2, False)
     pair_gradient(in_a, 0)
     back_through(0, x_full, 0, 0, True)
-
-
-def main_call(images, *operands):
-    n = images
+    sources = (g_attn, g_wide, g_down, g_pair, g_small)
+    arrived = (arrived_attn, arrived_wide, arrived_down, arrived_pair, arrived_small)
+    outs = (sum_attn, sum_wide, sum_down, sum_pair, sum_small)
+    sems = (sems_attn, sems_wide, sems_down, sems_pair, sems_small)
+    pieces = [Piece(*parts, stages) for parts in zip(sources, arrived, outs, sems)]
+    last = 2 * len(stages)
+    for t in range(last + len(pieces)):
+        for i, piece in enumerate(pieces):
+            if 0 <= t - i <= last:
+                piece.step(t - i)
+
+
+def main_call(dp_size, *operands):
+    n = operands[1].shape[1]
+    stages = (dp_size - 1).bit_length() + 1
     vm = pltpu.VMEM
     full = (n, 2, RES, HALF, C1)
     planes = (n, 4, RES + 2, HALF, C1)
     wide = HALF_CHANNELS
     square = (n, HALF * HALF, wide)
-    scratch = [
+    moved = [vm(v.shape, v.dtype) for v in operands[1:4] + operands[5:11]]
+    scratch = moved + [vm(shape, f32) for shape in PIECES]
+    scratch += [vm((arrived_rows(rows, stages), lanes), f32) for rows, lanes in PIECES]
+    scratch += [pltpu.SemaphoreType.DMA((2, 2 * stages)) for _ in PIECES]
+    scratch += [
+        vm((stages + 1, NB, 128), f32),
+        vm((stages, NB, 128), f32),
+        pltpu.SemaphoreType.DMA((2, 3)),
+        pltpu.SemaphoreType.DMA((3,)),
+        pltpu.SemaphoreType.DMA((2, stages)),
+        pltpu.SemaphoreType.DMA((6,)),
         vm((2, 12 * C1, 2 * C1), bf16),
         vm((2, 2 * C1, 12 * C1), bf16),
         vm((9 * C1, wide), bf16),
@@ -776,16 +846,20 @@
         vm((3, n, 4, 8, wide), f32),
     ]
     whole = pl.BlockSpec(memory_space=pltpu.VMEM)
+    anywhere = pl.BlockSpec(memory_space=pl.ANY)
     return pl.pallas_call(
-        main_kernel,
-        out_shape=[
-            jax.ShapeDtypeStruct(shape, f32)
-            for shape in PIECES
-        ],
-        in_specs=[pl.BlockSpec(memory_space=pltpu.SMEM)] + [whole] * 13,
-        out_specs=[whole] * 5,
+        functools.partial(main_kernel, dp_size),
+        out_shape=[jax.ShapeDtypeStruct(shape, f32) for shape in PIECES + ((NB, 128),)],
+        in_specs=[pl.BlockSpec(memory_space=pltpu.SMEM)]
+        + [anywhere] * 3
+        + [whole]
+        + [anywhere] * 6
+        + [whole] * 3,
+        out_specs=[whole] * (len(PIECES) + 1),
         scratch_shapes=scratch,
-        compiler_params=pltpu.CompilerParams(vmem_limit_bytes=VMEM_LIMIT),
+        compiler_params=pltpu.CompilerParams(
+            collective_id=0, has_side_effects=True, vmem_limit_bytes=VMEM_LIMIT
+        ),
         cost_estimate=pl.CostEstimate(flops=8 * 10**9, bytes_accessed=12 * 10**6, transcendentals=0),
     )(*operands)
 
@@ -833,63 +907,34 @@
     )
 
 
-def images_kernel(
-    dp_size, buckets, features, target, mask, mask_in, x_out, target_out, mask_out, counts_out,
-    totals, arrived, sems, local_sems, count_sems,
-):
-    stages = partners(dp_size)
-    dp = lax.axis_index("dp")
-    sp = lax.axis_index("sp")
-    greet(stages)
-    copies = [
-        send(source.at[1 - sp], out.at[sp], sems, i, (dp, 1 - sp))
-        for i, (source, out) in enumerate(((features, x_out), (target, target_out), (mask, mask_out)))
-    ]
-    for copy in copies:
-        copy.start()
-    keeps = [
-        pltpu.make_async_copy(source.at[sp], out.at[sp], local_sems.at[i])
-        for i, (source, out) in enumerate(((features, x_out), (target, target_out), (mask, mask_out)))
-    ]
-    for copy in keeps:
-        copy.start()
-    rows = lax.broadcasted_iota(jnp.int32, (NB, 128), 0)
-    counted = jnp.zeros((NB, 128), f32)
-    images = mask_in.shape[1]
-    for i in range(2 * images):
-        pixels = mask_in[i // images, i % images].astype(f32)
-        number = jnp.sum(jnp.sum(pixels, axis=0, keepdims=True), axis=1, keepdims=True)
-        counted = counted + jnp.where(rows == buckets[i], number, 0.0)
-    totals[0] = counted
-    for s, (_, other) in enumerate(stages):
-        copy = send(totals.at[s], arrived.at[s], count_sems, s, other)
-        copy.start()
-        copy.wait()
-        totals[s + 1] = totals[s] + arrived[s]
-    counts_out[...] = totals[len(stages)]
-    for copy in keeps + copies:
-        copy.wait()
-
-
-def images_call(dp_size, buckets, features, target, mask):
-    stages = (dp_size - 1).bit_length() + 1
-    anywhere = pl.BlockSpec(memory_space=pl.ANY)
-    whole = pl.BlockSpec(memory_space=pltpu.VMEM)
-    shapes = [jax.ShapeDtypeStruct(v.shape, v.dtype) for v in (features, target, mask)]
-    return pl.pallas_call(
-        functools.partial(images_kernel, dp_size),
-        out_shape=shapes + [jax.ShapeDtypeStruct((NB, 128), f32)],
-        in_specs=[pl.BlockSpec(memory_space=pltpu.SMEM)] + [anywhere] * 3 + [whole],
-        out_specs=[anywhere] * 3 + [whole],
-        scratch_shapes=[
-            pltpu.VMEM((stages + 1, NB, 128), f32),
-            pltpu.VMEM((stages, NB, 128), f32),
-            pltpu.SemaphoreType.DMA((2, 3)),
-            pltpu.SemaphoreType.DMA((3,)),
-            pltpu.SemaphoreType.DMA((2, stages)),
-        ],
-        compiler_params=pltpu.CompilerParams(collective_id=0, has_side_effects=True),
-    )(buckets, features, target, mask, mask)
+class Counting:
+    def __init__(self, buckets, mask, totals, arrived, sems, stages):
+        rows = lax.broadcasted_iota(jnp.int32, (NB, 128), 0)
+        counted = jnp.zeros((NB, 128), f32)
+        images = mask.shape[1]
+        for i in range(2 * images):
+            pixels = mask[i // images, i % images].astype(f32)
+            number = jnp.sum(jnp.sum(pixels, axis=0, keepdims=True), axis=1, keepdims=True)
+            counted = counted + jnp.where(rows == buckets[i], number, 0.0)
+        totals[0] = counted
+        self.totals, self.arrived, self.sems, self.stages = totals, arrived, sems, stages
+        self.copies = []
+
+    def step(self):
+        done = len(self.copies)
+        if done:
+            self.copies[-1].wait()
+            self.totals[done] = self.totals[done - 1] + self.arrived[done - 1]
+        if done < len(self.stages):
+            copy = send(self.totals.at[done], self.arrived.at[done], self.sems, done, self.stages[done][1])
+            copy.start()
+            self.copies.append(copy)
+
+    def finish(self, counts):
+        while len(self.copies) < len(self.stages):
+            self.step()
+        self.step()
+        counts[...] = self.totals[len(self.stages)]
 
 
 def chunk_of(rows):
@@ -981,35 +1026,6 @@
         rows = rows // 2 if rows % 16 == 0 else rows
         needed += rows
     return needed
-
-
-def sum_kernel(dp_size, *refs):
-    count = len(PIECES)
-    sources, outs, arrived, sems = (refs[i * count : (i + 1) * count] for i in range(4))
-    stages = partners(dp_size)
-    greet(stages)
-    pieces = [Piece(*parts, stages) for parts in zip(sources, arrived, outs, sems)]
-    last = 2 * len(stages)
-    for t in range(last + count):
-        for i, piece in enumerate(pieces):
-            if 0 <= t - i <= last:
-                piece.step(t - i)
-
-
-def sum_call(dp_size, partial):
-    stages = (dp_size - 1).bit_length() + 1
-    whole = pl.BlockSpec(memory_space=pltpu.VMEM)
-    return pl.pallas_call(
-        functools.partial(sum_kernel, dp_size),
-        out_shape=[jax.ShapeDtypeStruct(shape, f32) for shape in PIECES],
-        in_specs=[whole] * len(PIECES),
-        out_specs=[whole] * len(PIECES),
-        scratch_shapes=[pltpu.VMEM((arrived_rows(rows, stages), lanes), f32) for rows, lanes in PIECES]
-        + [pltpu.SemaphoreType.DMA((2, 2 * stages)) for _ in PIECES],
-        compiler_params=pltpu.CompilerParams(
-            collective_id=1, has_side_effects=True, vmem_limit_bytes=VMEM_LIMIT
-        ),
-    )(*partial)
 
 
 def adamw(weight, grad, first, second, rate):
@@ -1124,13 +1140,6 @@
     def head_rows(tensor):
         return jnp.transpose(tensor, (0, 1, 3, 2)).reshape(9, 3, HALF_CHANNELS)
 
-    images_in = images_call(
-        dp_size,
-        buckets,
-        halves(features),
-        halves(jnp.transpose(target, (0, 3, 1, 2))),
-        halves(pixel_mask),
-    )
     params = (
         flat(conv_pair),
         flat(down_conv),
@@ -1164,8 +1173,16 @@
         norm_wide_sq,
         time_bias_sq,
     )
-    partial = main_call(images, buckets, *images_in, *params)
-    summed = sum_call(dp_size, partial)
+    masks = halves(pixel_mask)
+    *summed, counts = main_call(
+        dp_size,
+        buckets,
+        halves(features),
+        halves(jnp.transpose(target, (0, 3, 1, 2))),
+        masks,
+        masks,
+        *params,
+    )
     results = update_call(summed, list(zip(params, firsts, seconds)))
     shaped = []
     for member, like in enumerate((conv_pair, down_conv, conv_wide, skip_proj, attn_proj)):
@@ -1173,7 +1190,7 @@
     for v in results[15:18]:
         shaped.append(jnp.transpose(v.reshape(3, 3, 3, HALF_CHANNELS), (0, 1, 3, 2)))
     shaped.extend(results[18:27])
-    return (results[27][0, 0], images_in[3][:, 0]) + tuple(shaped)
+    return (results[27][0, 0], counts[:, 0]) + tuple(shaped)
 
 
 def solution(mesh):

time: 159 us -> 146 us (0.918)
  Pallas kernels: 156 us -> 143 us
    pallas_call x3 -> x1, Pallas kernels: 136 us -> 124 us  [main_call(): pl.pallas_call(functools.partial(main_kernel, dp_size), out_shape=[jax.Sh...]
where the time goes in v1:
time: 146 us; the launch traced here: 145 us
  Pallas kernels  143 us (98%)
    pallas_call x1, Pallas kernels, main_call(): pl.pallas_call(functools.partial(main_kernel, dp_size), out_shape=[jax.Sh...  124 us
    pallas_call x1, Pallas kernels, update_call(): pl.pallas_call(update_kernel, out_shape=[jax.ShapeDtypeStruct(v.shape, f3...  19.8 us

profile of v1, /device:TPU:0, one launch (start us, length us, event | category | flops | bytes accessed | tf_op | source)
XLA Modules:
  0.0 145.5 jit_solution(1436239422858256279)
XLA Ops:
  0.7 123.5 %shard_map.518 = (f32[2048,128]{1,0:T(8,128)}, f32[4608,128]{1,0:T(8,128)}, f32[2560,128]{1,0:T(8,128)}, f32[2304,128]{1,0:T(8,128)}, f32[128,256]{1,0:T(8,128)}, /*index=5*/f32[8,128]{1,0:T(8,128)}) custom-call(s32[4]{0:T(128)} %buckets.1, bf16[2,2,16,32,128]{4,3,2,1,0:T(8,128)(2,1)} %bitcast.68, bf16[2,2,3,16,32]{4,3,2,1,0:T(8,128)(2,1)} %bitcast.69, ...), custom_call_target="tpu_custom_call" | custom-call | flops 8000000000 | bytes 12000000 | tf_op jit(solution)/shard_map/pallas_call | solution.py:850
  124.2 1.3 slice_reduce_fusion
  125.5 19.8 %shard_map.519 = (f32[2304,128]{1,0:T(8,128)}, f32[2304,128]{1,0:T(8,128)}, f32[2304,128]{1,0:T(8,128)}, f32[1152,256]{1,0:T(8,128)}, f32[1152,256]{1,0:T(8,128)...) custom-call(f32[2048,128]{1,0:T(8,128)} %get-tuple-element.63.refs_0, ...), custom_call_target="tpu_custom_call" | custom-call | tf_op jit(solution)/shard_map/pallas_call | solution.py:1088

commit v2 on v1

--- a/solution.py
+++ b/solution.py
@@ -252,29 +252,39 @@
 HEAD_ROWS = 72
 WIDE_NORM_ROW = 72
 LOSS_ROW = 78
-NARROW_NORM_ROW = 80
-TIME_WIDE_ROW = 88
-TIME_NARROW_ROW = 96
-SMALL_ROWS = 128
+TIME_WIDE_ROW = 80
+SMALL_ROWS = 96
+TIME_NARROW_ROW = 8
+LATE_ROWS = 16
 SKIP_ROW = 18 * C1
-PIECES = (
-    (8 * HALF_CHANNELS, 128),
-    (18 * HALF_CHANNELS, 128),
-    (20 * C1, 128),
-    (18 * C1, 128),
-    (SMALL_ROWS, HALF_CHANNELS),
-)
+ATTN_ROWS = 8 * HALF_CHANNELS
+WIDE_ROWS = 18 * HALF_CHANNELS
+DOWN_ROWS = 20 * C1
+PAIR_ROWS = 9 * C1
+GRADS = (ATTN_ROWS, WIDE_ROWS, DOWN_ROWS, PAIR_ROWS, PAIR_ROWS)
+TILE = 16
+
+
+def padded(rows, devices, tile):
+    return -(-rows // (devices * tile)) * devices * tile
+
+
+def coded_rows(rows, devices):
+    return padded(rows, devices, TILE) + devices * TILE
 
 
 def main_kernel(
     dp_size,
     buckets, features, target_rows, mask_rows, mask_local, pair_all, down_all, wide_all, skip_all, attn_all, head_all,
     gains_narrow, gains_wide, time_bias,
-    sum_attn, sum_wide, sum_down, sum_pair, sum_small, counts,
-    x_in, target, mask, pair, down, wide, skip, attn, head, g_attn, g_wide, g_down, g_pair, g_small,
-    arrived_attn, arrived_wide, arrived_down, arrived_pair, arrived_small,
-    sems_attn, sems_wide, sems_down, sems_pair, sems_small,
-    totals, arrived_totals, image_sems, local_sems, count_sems, weight_sems,
+    sum_attn, sum_wide, sum_down, sum_pair_b, sum_pair_a, sum_small, sum_late, counts,
+    x_in, target, mask, pair, down, wide, skip, attn, head,
+    g_attn, g_wide, g_down, g_pair_b, g_pair_a, g_rows,
+    out_attn, out_wide, out_down, out_pair_b, out_pair_a,
+    in_attn, in_wide, in_down, in_pair_b, in_pair_a, in_small,
+    sems_attn, sems_wide, sems_down, sems_pair_b, sems_pair_a, sems_small,
+    g_small, g_late,
+    totals, arrived_totals, late_totals, arrived_late, image_sems, local_sems, count_sems, late_sems, weight_sems,
     pair_fwd, pair_bwd, down_fwd, down_bwd, wide_fwd, wide_bwd, skip_low, attn_low, head_low,
     x_full, h1_full, xs_full, dy_full, in_a, in_b, in_g, flat,
     cells_c, cells_d, cells_g, fs_low, dfs, h3, x2, x3, n5, qkv, probs, probs_low, att, a6, dwide, dout, dqkv, dnarrow,
@@ -293,13 +303,13 @@
             )
         )
     ]
-    stages = partners(dp_size)
-    greet(stages)
+    links = Links(dp_size)
+    links.greet()
     here = (lax.axis_index("dp"), 1 - lax.axis_index("sp"))
     moved = ((features, x_in), (target_rows, target), (mask_rows, mask))
     side = lax.axis_index("sp")
     arrivals = [
-        send(source.at[1 - side], out.at[side], image_sems, i, here) for i, (source, out) in enumerate(moved)
+        send(source.at[1 - side], out.at[side], image_sems, i, i, here) for i, (source, out) in enumerate(moved)
     ]
     for copy in arrivals:
         copy.start()
@@ -333,12 +343,28 @@
     def row_of(ref, which, n, kind):
         return ref[which, n, kind, 0:1, :]
 
-    counting = Counting(buckets, mask_local, totals, arrived_totals, count_sems, stages)
+    counting = Exchange(count_pixels(buckets, mask_local), totals, arrived_totals, count_sems, links.brief)
     counting.step()
+    sources = (g_attn, g_wide, g_down, g_pair_b, g_pair_a, g_rows)
+    outgoing = (out_attn, out_wide, out_down, out_pair_b, out_pair_a, None)
+    incoming = (in_attn, in_wide, in_down, in_pair_b, in_pair_a, in_small)
+    outs = (sum_attn, sum_wide, sum_down, sum_pair_b, sum_pair_a, sum_small)
+    sems = (sems_attn, sems_wide, sems_down, sems_pair_b, sems_pair_a, sems_small)
+    orders = (links.brief, links.full, links.brief, links.brief, links.brief, links.brief)
+    pieces = dict(zip(PIECE_NAMES, (Piece(*parts) for parts in zip(sources, outgoing, incoming, outs, sems, orders))))
+
+    def advance(point):
+        for name in SCHEDULE.get(point, ()):
+            pieces[name].step()
+
+    for rows, ref in zip(GRADS + (2 * SMALL_ROWS,), sources):
+        if ref.shape[0] > rows:
+            ref[rows:, :] = jnp.zeros((ref.shape[0] - rows, 128), f32)
     for copy in loads:
         copy.wait()
     prepare_weights(pair, down, wide, skip, attn, head, pair_fwd, pair_bwd, down_fwd, down_bwd, wide_fwd, wide_bwd, skip_low, attn_low, head_low)
     g_small[...] = jnp.zeros(g_small.shape, f32)
+    g_late[...] = jnp.zeros(g_late.shape, f32)
     for planes in (in_a, in_b, in_g):
         edge = jnp.zeros((images, 4, HALF, C1), bf16)
         planes[:, :, 0] = edge
@@ -604,6 +630,7 @@
         6 * HALF_CHANNELS,
         mm_tn(att[...].reshape(-1, HALF_CHANNELS), dout[...].reshape(-1, HALF_CHANNELS)),
     )
+    advance("attn")
     for n in range(images):
         dy = mm_nt(dqkv[n], attn_low[:, : 3 * HALF_CHANNELS])
         v = x2[n]
@@ -625,8 +652,10 @@
                 product[k * HALF_CHANNELS : (k + 1) * HALF_CHANNELS],
             )
     keep_columns(g_down, SKIP_ROW, mm_tn(fs_low[...].reshape(-1, C1), center))
+    advance("wide")
     dfs[...] = mm_nt(center, skip_low[...]).reshape(dfs.shape)
     out = mm_nt(cell_input(cells_g, range(3)), wide_bwd[...])
+    advance("conv_d")
     bucket_rows = lax.broadcasted_iota(jnp.int32, (NB, HALF_CHANNELS), 0)
     time_wide = jnp.zeros((NB, HALF_CHANNELS), f32)
     for n in range(images):
@@ -644,11 +673,16 @@
         store_shifted(cells_g, n, 0, grad.reshape(HALF, HALF, HALF_CHANNELS))
     g_small[TIME_WIDE_ROW : TIME_WIDE_ROW + NB, :] = time_wide
 
+    for c in range(2):
+        g_rows[c * SMALL_ROWS : (c + 1) * SMALL_ROWS, :] = g_small[:, c * 128 : (c + 1) * 128]
+    advance("gn_d")
+
     center = cells_g[:, 1, 1 : HALF + 1].reshape(-1, HALF_CHANNELS)
     for dy in range(3):
         product = mm_tn(cell_input(cells_c, [dy]), center)
         for k in range(3):
             keep_columns(g_down, (dy * 3 + k) * 2 * C1, product[k * C1 : (k + 1) * C1])
+    advance("down")
     dnarrow[...] = mm_nt(cell_input(cells_g, range(3)), down_bwd[...]).reshape(dnarrow.shape)
 
     def up_parts(ref, n, i, size):
@@ -690,8 +724,9 @@
         gain, shift, ca, cb, cd = norm_grad_coefs(
             sum_dy, sum_dyv, gain_n(4), coef_n[2, n, 2], coef_n[2, n, 3], full_pixels
         )
-        g_small[NARROW_NORM_ROW + 4 : NARROW_NORM_ROW + 5, :C1] += gain[0:1, :]
-        g_small[NARROW_NORM_ROW + 5 : NARROW_NORM_ROW + 6, :C1] += shift[0:1, :]
+        g_late[4:5, :] += gain[0:1, :]
+        g_late[5:6, :] += shift[0:1, :]
+        advance("t%da" % n)
 
         def finish(i):
             parts = up_parts(dfs, n, i, size)
@@ -704,7 +739,10 @@
 
         each(4, finish)
 
-    each(images, third_norm)
+    advance("narrow")
+    for n in range(images):
+        third_norm(n)
+        advance("t%db" % n)
 
     def pair_gradient(planes, member):
         products = None
@@ -720,14 +758,15 @@
                 blocks.append(wide_part[:, (jj % 2) * 3 * C1 : (jj % 2 + 1) * 3 * C1])
             both = blocks[0] + blocks[1]
             for k in range(3):
-                row = (member * 9 + dy * 3 + k) * C1
-                g_pair[row : row + C1, :] = both[:, k * C1 : (k + 1) * C1].T
+                row = (dy * 3 + k) * C1
+                (g_pair_b if member else g_pair_a)[row : row + C1, :] = both[:, k * C1 : (k + 1) * C1].T
 
     def back_through(member, values, which, gain_row, last):
         for b in range(2):
             out = mm_nt(pair_input(in_g, b, range(4)), pair_bwd[member])
             for n in range(images):
                 dy_full[n, b, pl.ds(0, RES)] = pair_rows(out, n)
+        advance("b%dc" % member)
         bucket_rows = lax.broadcasted_iota(jnp.int32, (NB, C1), 0)
 
         def image(n):
@@ -750,9 +789,8 @@
             gain, shift, ca, cb, cd = norm_grad_coefs(
                 sum_dy, sum_dyv, gain_n(gain_row), coef_n[which, n, 2], coef_n[which, n, 3], full_pixels
             )
-            row = NARROW_NORM_ROW + gain_row
-            g_small[row : row + 1, :C1] += gain[0:1, :]
-            g_small[row + 1 : row + 2, :C1] += shift[0:1, :]
+            g_late[gain_row : gain_row + 1, :] += gain[0:1, :]
+            g_late[gain_row + 1 : gain_row + 2, :] += shift[0:1, :]
             if last:
                 return
 
@@ -766,45 +804,60 @@
                 return carry
 
             sums = total(lax.fori_loop(0, steps, finish, zero_n))
-            g_small[TIME_NARROW_ROW : TIME_NARROW_ROW + NB, :C1] += jnp.where(
+            g_late[TIME_NARROW_ROW : TIME_NARROW_ROW + NB, :] += jnp.where(
                 bucket_rows == bucket(n), sums, 0.0
             )
 
-        each(images, image)
+        for n in range(images):
+            image(n)
+            advance("b%di%d" % (member, n))
 
     pair_gradient(in_b, 1)
+    advance("pair_b")
     back_through(1, h1_full, 1, 2, False)
     pair_gradient(in_a, 0)
+    advance("pair_a")
     back_through(0, x_full, 0, 0, True)
-    sources = (g_attn, g_wide, g_down, g_pair, g_small)
-    arrived = (arrived_attn, arrived_wide, arrived_down, arrived_pair, arrived_small)
-    outs = (sum_attn, sum_wide, sum_down, sum_pair, sum_small)
-    sems = (sems_attn, sems_wide, sems_down, sems_pair, sems_small)
-    pieces = [Piece(*parts, stages) for parts in zip(sources, arrived, outs, sems)]
-    last = 2 * len(stages)
-    for t in range(last + len(pieces)):
-        for i, piece in enumerate(pieces):
-            if 0 <= t - i <= last:
-                piece.step(t - i)
+    pieces["late"] = Exchange(g_late[...], late_totals, arrived_late, late_sems, links.brief)
+    advance("end")
+    while any(piece.left() for piece in pieces.values()):
+        for name, piece in pieces.items():
+            if piece.left():
+                piece.step()
+    sum_late[...] = late_totals[len(links.brief)]
 
 
 def main_call(dp_size, *operands):
     n = operands[1].shape[1]
-    stages = (dp_size - 1).bit_length() + 1
+    devices = 2 * dp_size
+    counts = group_sizes(dp_size)
+    orders = (counts[1], counts[0]) + (counts[1],) * 4
+    grads = [padded(rows, devices, TILE) for rows in GRADS]
+    sums = [(coded_rows(rows, devices), jnp.int16) for rows in GRADS]
+    sums.append((padded(2 * SMALL_ROWS, devices, 8), f32))
+    spaces = [message_rows(rows, order, TILE) for rows, order in zip(grads, orders)]
+    small_space = message_rows(sums[-1][0], orders[-1], 0)
+    stages = sum(size - 1 for size in counts[1])
     vm = pltpu.VMEM
     full = (n, 2, RES, HALF, C1)
     planes = (n, 4, RES + 2, HALF, C1)
     wide = HALF_CHANNELS
     square = (n, HALF * HALF, wide)
     moved = [vm(v.shape, v.dtype) for v in operands[1:4] + operands[5:11]]
-    scratch = moved + [vm(shape, f32) for shape in PIECES]
-    scratch += [vm((arrived_rows(rows, stages), lanes), f32) for rows, lanes in PIECES]
-    scratch += [pltpu.SemaphoreType.DMA((2, 2 * stages)) for _ in PIECES]
+    scratch = moved + [vm((rows, 128), f32) for rows in grads + [sums[-1][0]]]
+    scratch += [vm((rows, 128), jnp.int16) for rows in spaces]
+    scratch += [vm((rows, 128), jnp.int16) for rows in spaces] + [vm((small_space, 128), f32)]
+    scratch += [pltpu.SemaphoreType.DMA((2, 2 * sum(size - 1 for size in order))) for order in orders]
     scratch += [
-        vm((stages + 1, NB, 128), f32),
-        vm((stages, NB, 128), f32),
+        vm((SMALL_ROWS, wide), f32),
+        vm((LATE_ROWS, C1), f32),
+        vm((len(counts[1]) + 1, NB, 128), f32),
+        vm((sum(counts[1]), NB, 128), f32),
+        vm((len(counts[1]) + 1, LATE_ROWS, 128), f32),
+        vm((sum(counts[1]), LATE_ROWS, 128), f32),
         pltpu.SemaphoreType.DMA((2, 3)),
         pltpu.SemaphoreType.DMA((3,)),
+        pltpu.SemaphoreType.DMA((2, stages)),
         pltpu.SemaphoreType.DMA((2, stages)),
         pltpu.SemaphoreType.DMA((6,)),
         vm((2, 12 * C1, 2 * C1), bf16),
@@ -849,13 +902,13 @@
     anywhere = pl.BlockSpec(memory_space=pl.ANY)
     return pl.pallas_call(
         functools.partial(main_kernel, dp_size),
-        out_shape=[jax.ShapeDtypeStruct(shape, f32) for shape in PIECES + ((NB, 128),)],
+        out_shape=[jax.ShapeDtypeStruct((rows, 128), dtype) for rows, dtype in sums + [(LATE_ROWS, f32), (NB, f32)]],
         in_specs=[pl.BlockSpec(memory_space=pltpu.SMEM)]
         + [anywhere] * 3
         + [whole]
         + [anywhere] * 6
         + [whole] * 3,
-        out_specs=[whole] * (len(PIECES) + 1),
+        out_specs=[whole] * (len(sums) + 2),
         scratch_shapes=scratch,
         compiler_params=pltpu.CompilerParams(
             collective_id=0, has_side_effects=True, vmem_limit_bytes=VMEM_LIMIT
@@ -864,168 +917,290 @@
     )(*operands)
 
 
-def partners(dp_size):
-    dp = lax.axis_index("dp")
-    sp = lax.axis_index("sp")
-
-    def flip(k):
-        unit = 1 << k
-        side = (dp // unit) % 2
-        return side, (dp + unit * (1 - 2 * side), sp)
-
-    core, near = flip(0), flip(1)
-    second = core[0]
-
-    def pick(first, other):
-        return first + second * (other - first)
-
-    stages = [
-        core,
-        (pick(near[0], sp), (pick(near[1][0], dp), pick(sp, 1 - sp))),
-        (pick(sp, near[0]), (pick(dp, near[1][0]), pick(1 - sp, sp))),
-    ]
-    for k in range(2, (dp_size - 1).bit_length()):
-        stages.append(flip(k))
-    return stages
-
-
-def greet(stages):
-    barrier = pltpu.get_barrier_semaphore()
-    for _, other in stages:
-        pl.semaphore_signal(barrier, inc=1, device_id=other, device_id_type=MESH)
-    pl.semaphore_wait(barrier, len(stages))
-
-
-def send(source, target, sems, index, other):
+PIECE_NAMES = ("attn", "wide", "down", "pair_b", "pair_a", "small")
+SCHEDULE = {
+    "attn": ("attn",),
+    "wide": ("wide", "attn"),
+    "gn_d": ("small", "wide"),
+    "down": ("down", "small"),
+    "t0a": ("down", "attn"),
+    "t1a": ("wide",),
+    "t1b": ("small",),
+    "pair_b": ("pair_b",),
+    "b1c": ("attn",),
+    "b1i0": ("pair_b", "down", "small", "wide"),
+    "pair_a": ("pair_a",),
+    "b0c": ("attn",),
+    "b0i0": ("pair_a", "pair_b"),
+    "end": ("late", "down", "small", "late", "wide", "attn", "pair_b", "attn", "pair_a", "down", "small", "late", "small", "wide", "pair_b", "pair_a", "down", "late", "wide", "down", "pair_a", "pair_b", "pair_b", "wide", "wide", "pair_a", "pair_a"),
+}
+
+
+def group_sizes(dp_size):
+    bits = (dp_size - 1).bit_length()
+    far = []
+    k = 2
+    while k < bits:
+        far.append(1 << min(2, bits - k))
+        k += 2
+    return [2, 2, 2] + far, [2, 4] + far
+
+
+class Links:
+    def __init__(self, dp_size):
+        dp = lax.axis_index("dp")
+        sp = lax.axis_index("sp")
+        core = dp % 2
+        near = (dp // 2) % 2
+
+        def along(unit, size):
+            place = (dp // unit) % size
+            return place, [(dp + unit * ((place + r) % size - place), sp) for r in range(1, size)]
+
+        def pick(first, other):
+            return first + core * (other - first)
+
+        across = (dp, 1 - sp)
+        beside = (dp + 2 * (1 - 2 * near), sp)
+        second = (pick(near, sp), [(pick(beside[0], dp), pick(sp, 1 - sp))])
+        third = (pick(sp, near), [(pick(dp, beside[0]), pick(1 - sp, sp))])
+        place = 2 * near + sp
+        square = []
+        for r in range(1, 4):
+            member = (place + r) % 4
+            square.append((dp + 2 * (member // 2 - near), member % 2))
+        far = []
+        unit = 4
+        for size in group_sizes(dp_size)[1][2:]:
+            far.append(along(unit, size))
+            unit *= size
+        self.full = [along(1, 2), second, third] + far
+        self.brief = [along(1, 2), (place, square)] + far
+        self.all = [other for _, others in self.brief for other in others]
+
+    def greet(self):
+        barrier = pltpu.get_barrier_semaphore()
+        for other in self.all:
+            pl.semaphore_signal(barrier, inc=1, device_id=other, device_id_type=MESH)
+        pl.semaphore_wait(barrier, len(self.all))
+
+
+def send(source, target, sems, index, landing, other):
     return pltpu.make_async_remote_copy(
         src_ref=source,
         dst_ref=target,
         send_sem=sems.at[0, index],
-        recv_sem=sems.at[1, index],
+        recv_sem=sems.at[1, landing],
         device_id=other,
         device_id_type=MESH,
     )
 
 
-class Counting:
-    def __init__(self, buckets, mask, totals, arrived, sems, stages):
-        rows = lax.broadcasted_iota(jnp.int32, (NB, 128), 0)
-        counted = jnp.zeros((NB, 128), f32)
-        images = mask.shape[1]
-        for i in range(2 * images):
-            pixels = mask[i // images, i % images].astype(f32)
-            number = jnp.sum(jnp.sum(pixels, axis=0, keepdims=True), axis=1, keepdims=True)
-            counted = counted + jnp.where(rows == buckets[i], number, 0.0)
-        totals[0] = counted
+class Exchange:
+    def __init__(self, value, totals, arrived, sems, stages):
+        totals[0] = value
         self.totals, self.arrived, self.sems, self.stages = totals, arrived, sems, stages
+        self.t = self.base = self.index = 0
         self.copies = []
 
+    def left(self):
+        return self.t <= len(self.stages)
+
     def step(self):
-        done = len(self.copies)
-        if done:
-            self.copies[-1].wait()
-            self.totals[done] = self.totals[done - 1] + self.arrived[done - 1]
-        if done < len(self.stages):
-            copy = send(self.totals.at[done], self.arrived.at[done], self.sems, done, self.stages[done][1])
+        if self.copies:
+            for copy in self.copies:
+                copy.wait()
+            size = len(self.copies) + 1
+            total_now = self.arrived[self.base]
+            for m in range(1, size):
+                total_now = total_now + self.arrived[self.base + m]
+            self.totals[self.t] = total_now
+            self.base += size
+            self.index += size - 1
+            self.copies = []
+        if self.t < len(self.stages):
+            place, others = self.stages[self.t]
+            mine = self.totals.at[self.t]
+            landing = self.arrived.at[self.base + place]
+            for r, other in enumerate(others):
+                copy = send(mine, landing, self.sems, self.index + r, self.index + len(others) - 1 - r, other)
+                copy.start()
+                self.copies.append(copy)
+            self.arrived[self.base + place] = self.totals[self.t]
+        self.t += 1
+
+    def finish(self, out):
+        while self.left():
+            self.step()
+        out[...] = self.totals[len(self.stages)]
+
+
+def count_pixels(buckets, mask):
+    rows = lax.broadcasted_iota(jnp.int32, (NB, 128), 0)
+    counted = jnp.zeros((NB, 128), f32)
+    images = mask.shape[1]
+    for i in range(2 * images):
+        pixels = mask[i // images, i % images].astype(f32)
+        number = jnp.sum(jnp.sum(pixels, axis=0, keepdims=True), axis=1, keepdims=True)
+        counted = counted + jnp.where(rows == buckets[i], number, 0.0)
+    return counted
+
+
+def chunk_of(rows):
+    return next(c for c in (128, 96, 80, 64, 48, 32, 16, 8) if rows % c == 0)
+
+
+def aligned(row, tile):
+    return row if isinstance(row, int) else pl.multiple_of(row, tile)
+
+
+def encode(source, first, rows, target, base):
+    size = chunk_of(rows)
+
+    def largest(i, carry):
+        v = jnp.abs(source[pl.ds(aligned(first + i * size, 8), size), :])
+        return jnp.maximum(carry, jnp.max(v.reshape(-1, 8, 128), axis=0))
+
+    bound = lax.fori_loop(0, rows // size, largest, jnp.zeros((8, 128), f32))
+    bound = jnp.max(bound, axis=0, keepdims=True)
+    power = jnp.floor(jnp.log2(jnp.maximum(bound, 1e-30))) + 1.0
+    scale = jnp.exp2(15.0 - power)
+
+    def step(i):
+        v = source[pl.ds(aligned(first + i * size, 8), size), :] * scale
+        v = jnp.clip(jnp.round(v), -32767.0, 32767.0)
+        target[pl.ds(aligned(base + i * size, TILE), size), :] = v.astype(jnp.int32).astype(jnp.int16)
+
+    each(rows // size, step)
+    target[pl.ds(aligned(base + rows, TILE), TILE), :] = jnp.broadcast_to(
+        power.astype(jnp.int32), (TILE, 128)
+    ).astype(jnp.int16)
+
+
+def decode(source, base, rows):
+    power = source[pl.ds(aligned(base + rows, TILE), TILE), :].astype(jnp.int32).astype(f32)
+    return jnp.exp2(power[0:1, :] - 15.0)
+
+
+def message_rows(rows, sizes, tile):
+    needed = 0
+    for size in sizes:
+        rows //= size
+        needed += (size - 1) * (rows + tile)
+    return needed
+
+
+class Piece:
+    def __init__(self, source, outgoing, arrived, out, sems, stages):
+        self.source, self.outgoing, self.arrived, self.out, self.sems = source, outgoing, arrived, out, sems
+        self.stages = stages
+        self.tile = 0 if outgoing is None else TILE
+        self.rows = source.shape[0]
+        self.first = 0
+        self.base = self.index = self.t = 0
+        self.copies = []
+        self.share = self.rows
+        for _, others in stages:
+            self.share //= len(others) + 1
+
+    def left(self):
+        return self.t <= 2 * len(self.stages)
+
+    def step(self):
+        count = len(self.stages)
+        if 0 < self.t <= count:
+            self.scatter_end(self.stages[self.t - 1])
+        elif self.t > count:
+            self.gather_end(self.stages[2 * count - self.t])
+        if self.t == count:
+            self.keep()
+        if self.t < count:
+            self.scatter_start(self.stages[self.t])
+        elif self.t < 2 * count:
+            self.gather_start(self.stages[2 * count - 1 - self.t])
+        self.t += 1
+
+    def scatter_start(self, stage):
+        place, others = stage
+        size = len(others) + 1
+        rows = self.rows // size
+        block = rows + self.tile
+        for r, other in enumerate(others):
+            part = self.first + ((place + r + 1) % size) * rows
+            if self.tile:
+                mine = self.base + r * block
+                encode(self.source, part, rows, self.outgoing, mine)
+                message = self.outgoing.at[pl.ds(mine, block)]
+            else:
+                message = self.source.at[pl.ds(aligned(part, 8), rows)]
+            landing = size - 2 - r
+            copy = send(
+                message,
+                self.arrived.at[pl.ds(self.base + landing * block, block)],
+                self.sems,
+                self.index + r,
+                self.index + landing,
+                other,
+            )
             copy.start()
             self.copies.append(copy)
 
-    def finish(self, counts):
-        while len(self.copies) < len(self.stages):
-            self.step()
-        self.step()
-        counts[...] = self.totals[len(self.stages)]
-
-
-def chunk_of(rows):
-    return next(c for c in (128, 96, 72, 64, 48, 40, 32, 24, 16, 8) if rows % c == 0)
-
-
-def add_rows(target, base, source, offset, rows):
-    size = chunk_of(rows)
-
-    def step(i):
-        here = pl.ds(pl.multiple_of(base + i * size, 8), size)
-        target[here, :] = target[here, :] + source[pl.ds(pl.multiple_of(offset + i * size, 8), size), :]
-
-    each(rows // size, step)
-
-
-class Piece:
-    def __init__(self, source, arrived, out, sems, stages):
-        self.source, self.arrived, self.out, self.sems, self.stages = source, arrived, out, sems, stages
-        rows = source.shape[0]
-        self.plan = []
-        base = 0
-        lowest = 0
-        for side, other in stages:
-            halved = rows % 16 == 0
-            rows = rows // 2 if halved else rows
-            self.plan.append((side, other, halved, rows, base, lowest))
-            lowest = lowest + side * rows if halved else lowest
-            base += rows
-        self.rows, self.lowest = rows, lowest
-        self.copies = {}
-
-    def region(self, s, side):
-        halved, rows = self.plan[s][2:4]
-        if s == 0:
-            ref, base = self.source, 0
+    def scatter_end(self, stage):
+        place, others = stage
+        size = len(others) + 1
+        rows = self.rows // size
+        block = rows + self.tile
+        for copy in self.copies:
+            copy.wait()
+        first = self.first + place * rows
+        scales = [decode(self.arrived, self.base + r * block, rows) if self.tile else 1.0 for r in range(size - 1)]
+        chunk = chunk_of(rows)
+
+        def add(i):
+            here = pl.ds(aligned(first + i * chunk, 8), chunk)
+            v = self.source[here, :]
+            for r, scale in enumerate(scales):
+                more = self.arrived[pl.ds(aligned(self.base + r * block + i * chunk, self.tile or 8), chunk), :]
+                v = v + (more.astype(jnp.int32).astype(f32) * scale if self.tile else more)
+            self.source[here, :] = v
+
+        each(rows // chunk, add)
+        self.first, self.rows = first, rows
+        self.base += (size - 1) * block
+        self.index += size - 1
+        self.copies = []
+
+    def keep(self):
+        block = self.share + self.tile
+        self.place = 0
+        for place, others in self.stages:
+            self.place = self.place * (len(others) + 1) + place
+        self.first = self.place * block
+        self.rows = block
+        if self.tile:
+            encode(self.source, self.place * self.share, self.share, self.out, self.first)
         else:
-            ref, base = self.arrived, self.plan[s - 1][4]
-        return ref, (base + side * rows if halved else base)
-
-    def scatter_start(self, s):
-        side, other, halved, rows, base, _ = self.plan[s]
-        ref, first = self.region(s, 1 - side)
-        copy = send(
-            ref.at[pl.ds(pl.multiple_of(first, 8), rows)],
-            self.arrived.at[pl.ds(base, rows)],
-            self.sems,
-            s,
-            other,
-        )
-        copy.start()
-        self.copies[s] = copy
-
-    def scatter_end(self, s):
-        side, other, halved, rows, base, _ = self.plan[s]
-        self.copies[s].wait()
-        ref, first = self.region(s, side)
-        add_rows(self.arrived, base, ref, first, rows)
-        if s + 1 == len(self.stages):
-            self.out[pl.ds(pl.multiple_of(self.lowest, 8), rows), :] = self.arrived[base : base + rows, :]
-
-    def gather_start(self, s):
-        side, other, halved, rows, base, lowest = self.plan[s]
-        if halved:
-            here = pl.ds(pl.multiple_of(lowest + side * rows, 8), rows)
-            copy = send(self.out.at[here], self.out.at[here], self.sems, len(self.stages) + s, other)
+            self.out[pl.ds(aligned(self.first, 8), block), :] = self.source[
+                pl.ds(aligned(self.first, 8), block), :
+            ]
+
+    def gather_start(self, stage):
+        place, others = stage
+        here = self.out.at[pl.ds(aligned(self.first, self.tile or 8), self.rows)]
+        for r, other in enumerate(others):
+            copy = send(here, here, self.sems, self.index + r, self.index + len(others) - 1 - r, other)
             copy.start()
-            self.copies[len(self.stages) + s] = copy
-
-    def gather_end(self, s):
-        if self.plan[s][2]:
-            self.copies[len(self.stages) + s].wait()
-
-    def step(self, t):
-        count = len(self.stages)
-        if 0 < t <= count:
-            self.scatter_end(t - 1)
-        elif t > count:
-            self.gather_end(2 * count - t)
-        if t < count:
-            self.scatter_start(t)
-        elif t < 2 * count:
-            self.gather_start(2 * count - 1 - t)
-
-
-def arrived_rows(rows, stages):
-    needed = 0
-    for _ in range(stages):
-        rows = rows // 2 if rows % 16 == 0 else rows
-        needed += rows
-    return needed
+            self.copies.append(copy)
+
+    def gather_end(self, stage):
+        place, others = stage
+        size = len(others) + 1
+        for copy in self.copies:
+            copy.wait()
+        self.copies = []
+        self.index += size - 1
+        self.first = self.first - place * self.rows
+        self.rows = self.rows * size
 
 
 def adamw(weight, grad, first, second, rate):
@@ -1036,19 +1211,35 @@
     return weight * (1.0 - rate * decay_rate) - scale * first / root, first, second
 
 
-def update_kernel(*refs):
-    g_attn, g_wide, g_down, g_pair, g_small = refs[:5]
-    members = [refs[5 + 3 * i : 8 + 3 * i] for i in range(9)]
-    outs = [refs[32 + 3 * i : 35 + 3 * i] for i in range(9)]
-    loss_out = refs[59]
-
-    def blocks(member, grad, block_rows, base, count):
+def update_kernel(devices, *refs):
+    count = len(GRADS)
+    coded, (g_small, g_late, counts), refs = refs[:count], refs[count : count + 3], refs[count + 3 :]
+    members = [refs[3 * i : 3 + 3 * i] for i in range(9)]
+    outs = [refs[27 + 3 * i : 30 + 3 * i] for i in range(9)]
+    loss_out, counts_out = refs[54:56]
+    grads = refs[56:]
+    g_attn, g_wide, g_down, g_pair_b, g_pair_a = grads
+    for source, grad in zip(coded, grads):
+        share = grad.shape[0] // devices
+
+        def shares(i, source=source, grad=grad, share=share):
+            base = i * (share + TILE)
+            v = source[pl.ds(aligned(base, TILE), share), :].astype(jnp.int32).astype(f32)
+            grad[pl.ds(aligned(i * share, 8), share), :] = v * decode(source, base, share)
+
+        each(devices, shares)
+
+    def small(row, rows, lanes):
+        parts = [g_small[c * SMALL_ROWS + row : c * SMALL_ROWS + row + rows, :] for c in range(lanes // 128)]
+        return parts[0] if len(parts) == 1 else jnp.concatenate(parts, axis=1)
+
+    def blocks(member, grad, block_rows, base, count, start=0):
         size = 64
 
         def step(i):
             block = i // (block_rows // size)
             row = (i % (block_rows // size)) * size
-            here = pl.ds(pl.multiple_of(block * block_rows + row, 8), size)
+            here = pl.ds(pl.multiple_of(start + block * block_rows + row, 8), size)
             columns = members[member][0].shape[1] // 128
             for c in range(columns):
                 lanes = slice(c * 128, (c + 1) * 128)
@@ -1064,33 +1255,34 @@
         for out, value in zip(outs[member], adamw(w, grad, m, v, rate)):
             out[index] = value
 
-    blocks(0, g_pair, C1, 0, 18)
+    blocks(0, g_pair_a, C1, 0, 9)
+    blocks(0, g_pair_b, C1, 0, 9, 9 * C1)
     blocks(1, g_down, C1, 0, 9)
     blocks(2, g_wide, HALF_CHANNELS, 0, 9)
     blocks(3, g_down, C1, SKIP_ROW, 1)
     blocks(4, g_attn, HALF_CHANNELS, 0, 1)
     for tap in range(9):
-        single(5, (tap,), g_small[tap * 8 : tap * 8 + 3, :], rate_matrix)
-    single(6, (slice(None), slice(None)), g_small[NARROW_NORM_ROW : NARROW_NORM_ROW + 6, :C1], rate_vector)
-    single(7, (slice(None), slice(None)), g_small[WIDE_NORM_ROW : WIDE_NORM_ROW + 6, :], rate_vector)
-    single(
-        8, (slice(None), slice(0, C1)), g_small[TIME_NARROW_ROW : TIME_NARROW_ROW + NB, :C1], rate_vector
-    )
-    single(
-        8, (slice(None), slice(C1, None)), g_small[TIME_WIDE_ROW : TIME_WIDE_ROW + NB, :], rate_vector
-    )
-    loss_out[...] = g_small[LOSS_ROW : LOSS_ROW + 1, :128]
-
-
-def update_call(grads, members):
+        single(5, (tap,), small(tap * 8, 3, HALF_CHANNELS), rate_matrix)
+    every = slice(None)
+    single(6, (every, every), g_late[:6, :], rate_vector)
+    single(7, (every, every), small(WIDE_NORM_ROW, 6, HALF_CHANNELS), rate_vector)
+    single(8, (every, slice(0, C1)), g_late[TIME_NARROW_ROW : TIME_NARROW_ROW + NB, :], rate_vector)
+    single(8, (every, slice(C1, None)), small(TIME_WIDE_ROW, NB, HALF_CHANNELS), rate_vector)
+    loss_out[...] = g_small[LOSS_ROW : LOSS_ROW + 1, :]
+    diagonal = lax.broadcasted_iota(jnp.int32, (NB, 128), 0) == lax.broadcasted_iota(jnp.int32, (NB, 128), 1)
+    counts_out[...] = jnp.sum(jnp.where(diagonal, counts[...], 0.0), axis=0, keepdims=True)[:, :NB]
+
+
+def update_call(devices, grads, members):
     whole = pl.BlockSpec(memory_space=pltpu.VMEM)
     flat = [v for member in members for v in member]
     return pl.pallas_call(
-        update_kernel,
+        functools.partial(update_kernel, devices),
         out_shape=[jax.ShapeDtypeStruct(v.shape, f32) for v in flat]
-        + [jax.ShapeDtypeStruct((1, 128), f32)],
-        in_specs=[whole] * (5 + len(flat)),
-        out_specs=[whole] * (len(flat) + 1),
+        + [jax.ShapeDtypeStruct((1, 128), f32), jax.ShapeDtypeStruct((1, NB), f32)],
+        in_specs=[whole] * (len(grads) + len(flat)),
+        out_specs=[whole] * (len(flat) + 2),
+        scratch_shapes=[pltpu.VMEM((padded(rows, devices, TILE), 128), f32) for rows in GRADS],
         compiler_params=pltpu.CompilerParams(vmem_limit_bytes=VMEM_LIMIT),
     )(*grads, *flat)
 
@@ -1174,7 +1366,7 @@
         time_bias_sq,
     )
     masks = halves(pixel_mask)
-    *summed, counts = main_call(
+    summed = main_call(
         dp_size,
         buckets,
         halves(features),
@@ -1183,14 +1375,14 @@
         masks,
         *params,
     )
-    results = update_call(summed, list(zip(params, firsts, seconds)))
+    results = update_call(2 * dp_size, summed, list(zip(params, firsts, seconds)))
     shaped = []
     for member, like in enumerate((conv_pair, down_conv, conv_wide, skip_proj, attn_proj)):
         shaped.extend(v.reshape(like.shape) for v in results[3 * member : 3 * member + 3])
     for v in results[15:18]:
         shaped.append(jnp.transpose(v.reshape(3, 3, 3, HALF_CHANNELS), (0, 1, 3, 2)))
     shaped.extend(results[18:27])
-    return (results[27][0, 0], counts[:, 0]) + tuple(shaped)
+    return (results[27][0, 0], results[28].reshape(NB)) + tuple(shaped)
 
 
 def solution(mesh):

time: 146 us -> 108 us (0.74)
  Pallas kernels: 143 us -> 107 us
    pallas_call x1, Pallas kernels: 124 us -> 85.2 us  [main_call(): pl.pallas_call(functools.partial(main_kernel, dp_size), out_shape=[jax.Sh...]
    pallas_call x1, Pallas kernels: 19.8 us -> 21.8 us  [update_call(): pl.pallas_call(functools.partial(update_kernel, devices), out_shape=[jax....]
where the time goes in v2:
time: 108 us
  Pallas kernels  107 us (99%)
    pallas_call x1, Pallas kernels, main_call(): pl.pallas_call(functools.partial(main_kernel, dp_size), out_shape=[jax.Sh...  85.2 us
    pallas_call x1, Pallas kernels, update_call(): pl.pallas_call(functools.partial(update_kernel, devices), out_shape=[jax....  21.8 us

profile of v2, /device:TPU:0, one launch (start us, length us, event | category | flops | bytes accessed | tf_op | source)
XLA Modules:
  0.0 107.8 jit_solution(5943132209122257328)
XLA Ops:
  0.7 85.2 %shard_map.518 = (s16[2560,128]{1,0:T(8,128)(2,1)}, s16[5120,128]{1,0:T(8,128)(2,1)}, s16[3072,128]{1,0:T(8,128)(2,1)}, s16[2048,128]{1,0:T(8,128)(2,1)}, s16[20...) custom-call(s32[4]{0:T(128)} %buckets.1, ...), custom_call_target="tpu_custom_call" | custom-call | flops 8000000000 | bytes 12000000 | tf_op jit(solution)/shard_map/pallas_call | solution.py:903
  85.9 21.8 %shard_map.519 = (f32[2304,128]{1,0:T(8,128)}, f32[2304,128]{1,0:T(8,128)}, f32[2304,128]{1,0:T(8,128)}, f32[1152,256]{1,0:T(8,128)}, f32[1152,256]{1,0:T(8,128)...) custom-call(s16[2560,128]{1,0:T(8,128)(2,1)} %get-tuple-element.66.r, ...), custom_call_target="tpu_custom_call" | custom-call | tf_op jit(solution)/shard_map/pallas_call | solution.py:1279

commit v3 on v2

--- a/solution.py
+++ b/solution.py
@@ -15,7 +15,8 @@
 NB = 8
 STEP = 10
 MESH = pl.DeviceIdType.MESH
-VMEM_LIMIT = 62 * 1024 * 1024
+MAIN_LIMIT = 41 * 1024 * 1024
+UPDATE_LIMIT = 26 * 1024 * 1024
 
 epsilon = 1e-05
 root_half = 0.7071067811865476
@@ -162,13 +163,13 @@
                 for a in range(2):
                     dy = jj - a
                     inside = 0 <= dy < 3
-                    row = (member * 9 + dy * 3 + k) * C1
-                    back = (member * 9 + (2 - dy) * 3 + (2 - k)) * C1
+                    row = (dy * 3 + k) * C1
+                    back = ((2 - dy) * 3 + (2 - k)) * C1
                     pair_fwd[member, block : block + C1, a * C1 : a * C1 + C1] = (
-                        pair[row : row + C1, :].astype(bf16) if inside else nothing
+                        pair[member][row : row + C1, :].astype(bf16) if inside else nothing
                     )
                     pair_bwd[member, a * C1 : a * C1 + C1, block : block + C1] = (
-                        pair[back : back + C1, :].astype(bf16) if inside else nothing
+                        pair[member][back : back + C1, :].astype(bf16) if inside else nothing
                     )
     wide_channels = HALF_CHANNELS
     for tap in range(9):
@@ -275,10 +276,10 @@
 
 def main_kernel(
     dp_size,
-    buckets, features, target_rows, mask_rows, mask_local, pair_all, down_all, wide_all, skip_all, attn_all, head_all,
-    gains_narrow, gains_wide, time_bias,
+    buckets, features, target_rows, mask_rows, pair_all, down_all, wide_all, skip_all, attn_all, head_all,
+    narrow_all, gains_all, time_all,
     sum_attn, sum_wide, sum_down, sum_pair_b, sum_pair_a, sum_small, sum_late, counts,
-    x_in, target, mask, pair, down, wide, skip, attn, head,
+    x_in, target, mask, down, wide, skip, attn, head, gains_narrow, gains_wide, time_bias, mask_local,
     g_attn, g_wide, g_down, g_pair_b, g_pair_a, g_rows,
     out_attn, out_wide, out_down, out_pair_b, out_pair_a,
     in_attn, in_wide, in_down, in_pair_b, in_pair_a, in_small,
@@ -294,17 +295,27 @@
         pltpu.make_async_copy(source, ref, weight_sems.at[i])
         for i, (source, ref) in enumerate(
             (
-                (pair_all, pair),
+                (pair_all.at[:PAIR_ROWS], g_pair_a.at[:PAIR_ROWS]),
+                (pair_all.at[PAIR_ROWS:], g_pair_b.at[:PAIR_ROWS]),
                 (down_all, down),
                 (wide_all, wide),
                 (skip_all, skip),
                 (attn_all, attn),
                 (head_all, head),
+                (narrow_all, gains_narrow),
+                (gains_all, gains_wide),
+                (time_all, time_bias),
+                (mask_rows, mask_local),
             )
         )
     ]
     links = Links(dp_size)
     links.greet()
+    for copy in loads[::-1]:
+        copy.start()
+    loads.pop().wait()
+    counted = count_pixels(buckets, mask_local)
+    links.meet()
     here = (lax.axis_index("dp"), 1 - lax.axis_index("sp"))
     moved = ((features, x_in), (target_rows, target), (mask_rows, mask))
     side = lax.axis_index("sp")
@@ -317,7 +328,7 @@
         pltpu.make_async_copy(source.at[side], out.at[side], local_sems.at[i])
         for i, (source, out) in enumerate(moved)
     ]
-    for copy in keeps + loads:
+    for copy in keeps:
         copy.start()
     images = x_in.shape[1]
     position = lax.axis_index("sp")
@@ -343,7 +354,7 @@
     def row_of(ref, which, n, kind):
         return ref[which, n, kind, 0:1, :]
 
-    counting = Exchange(count_pixels(buckets, mask_local), totals, arrived_totals, count_sems, links.brief)
+    counting = Exchange(counted, totals, arrived_totals, count_sems, links.brief)
     counting.step()
     sources = (g_attn, g_wide, g_down, g_pair_b, g_pair_a, g_rows)
     outgoing = (out_attn, out_wide, out_down, out_pair_b, out_pair_a, None)
@@ -362,7 +373,7 @@
             ref[rows:, :] = jnp.zeros((ref.shape[0] - rows, 128), f32)
     for copy in loads:
         copy.wait()
-    prepare_weights(pair, down, wide, skip, attn, head, pair_fwd, pair_bwd, down_fwd, down_bwd, wide_fwd, wide_bwd, skip_low, attn_low, head_low)
+    prepare_weights((g_pair_a, g_pair_b), down, wide, skip, attn, head, pair_fwd, pair_bwd, down_fwd, down_bwd, wide_fwd, wide_bwd, skip_low, attn_low, head_low)
     g_small[...] = jnp.zeros(g_small.shape, f32)
     g_late[...] = jnp.zeros(g_late.shape, f32)
     for planes in (in_a, in_b, in_g):
@@ -843,7 +854,7 @@
     planes = (n, 4, RES + 2, HALF, C1)
     wide = HALF_CHANNELS
     square = (n, HALF * HALF, wide)
-    moved = [vm(v.shape, v.dtype) for v in operands[1:4] + operands[5:11]]
+    moved = [vm(v.shape, v.dtype) for v in operands[1:4] + operands[5:] + operands[3:4]]
     scratch = moved + [vm((rows, 128), f32) for rows in grads + [sums[-1][0]]]
     scratch += [vm((rows, 128), jnp.int16) for rows in spaces]
     scratch += [vm((rows, 128), jnp.int16) for rows in spaces] + [vm((small_space, 128), f32)]
@@ -859,7 +870,7 @@
         pltpu.SemaphoreType.DMA((3,)),
         pltpu.SemaphoreType.DMA((2, stages)),
         pltpu.SemaphoreType.DMA((2, stages)),
-        pltpu.SemaphoreType.DMA((6,)),
+        pltpu.SemaphoreType.DMA((11,)),
         vm((2, 12 * C1, 2 * C1), bf16),
         vm((2, 2 * C1, 12 * C1), bf16),
         vm((9 * C1, wide), bf16),
@@ -899,22 +910,18 @@
         vm((3, n, 4, 8, wide), f32),
     ]
     whole = pl.BlockSpec(memory_space=pltpu.VMEM)
-    anywhere = pl.BlockSpec(memory_space=pl.ANY)
+    anywhere = pl.BlockSpec(memory_space=pltpu.HBM)
     return pl.pallas_call(
         functools.partial(main_kernel, dp_size),
         out_shape=[jax.ShapeDtypeStruct((rows, 128), dtype) for rows, dtype in sums + [(LATE_ROWS, f32), (NB, f32)]],
-        in_specs=[pl.BlockSpec(memory_space=pltpu.SMEM)]
-        + [anywhere] * 3
-        + [whole]
-        + [anywhere] * 6
-        + [whole] * 3,
+        in_specs=[pl.BlockSpec(memory_space=pltpu.SMEM)] + [anywhere] * 12,
         out_specs=[whole] * (len(sums) + 2),
         scratch_shapes=scratch,
         compiler_params=pltpu.CompilerParams(
-            collective_id=0, has_side_effects=True, vmem_limit_bytes=VMEM_LIMIT
+            collective_id=0, has_side_effects=True, vmem_limit_bytes=MAIN_LIMIT + 1536 * (sum(grads) - sum(GRADS))
         ),
         cost_estimate=pl.CostEstimate(flops=8 * 10**9, bytes_accessed=12 * 10**6, transcendentals=0),
-    )(*operands)
+    )(*[pltpu.with_memory_space_constraint(v, pltpu.HBM) for v in operands])
 
 
 PIECE_NAMES = ("attn", "wide", "down", "pair_b", "pair_a", "small")
@@ -982,7 +989,9 @@
         barrier = pltpu.get_barrier_semaphore()
         for other in self.all:
             pl.semaphore_signal(barrier, inc=1, device_id=other, device_id_type=MESH)
-        pl.semaphore_wait(barrier, len(self.all))
+
+    def meet(self):
+        pl.semaphore_wait(pltpu.get_barrier_semaphore(), len(self.all))
 
 
 def send(source, target, sems, index, landing, other):
@@ -1206,9 +1215,23 @@
 def adamw(weight, grad, first, second, rate):
     first = beta_one * first + (1.0 - beta_one) * grad
     second = beta_two * second + (1.0 - beta_two) * grad * grad
+    power = jnp.maximum(second * (1.0 / (1.0 - beta_two**STEP)), 1e-36)
+    root = power * lax.rsqrt(power) + adam_epsilon
     scale = rate / (1.0 - beta_one**STEP)
-    root = jnp.sqrt(second * (1.0 / (1.0 - beta_two**STEP))) + adam_epsilon
     return weight * (1.0 - rate * decay_rate) - scale * first / root, first, second
+
+
+PARTS = (
+    (2, 1, HALF_CHANNELS, 0, 3, 0),
+    (2, 1, HALF_CHANNELS, 6 * HALF_CHANNELS, 3, 3 * HALF_CHANNELS),
+    (2, 1, HALF_CHANNELS, 12 * HALF_CHANNELS, 3, 6 * HALF_CHANNELS),
+    (4, 0, HALF_CHANNELS, 0, 1, 0),
+    (1, 2, C1, 0, 9, 0),
+    (3, 2, C1, 18 * C1, 1, 0),
+    (0, 3, C1, 0, 9, 9 * C1),
+    (0, 4, C1, 0, 9, 0),
+)
+LARGE = 5
 
 
 def update_kernel(devices, *refs):
@@ -1217,50 +1240,64 @@
     members = [refs[3 * i : 3 + 3 * i] for i in range(9)]
     outs = [refs[27 + 3 * i : 30 + 3 * i] for i in range(9)]
     loss_out, counts_out = refs[54:56]
-    grads = refs[56:]
-    g_attn, g_wide, g_down, g_pair_b, g_pair_a = grads
-    for source, grad in zip(coded, grads):
-        share = grad.shape[0] // devices
-
-        def shares(i, source=source, grad=grad, share=share):
-            base = i * (share + TILE)
-            v = source[pl.ds(aligned(base, TILE), share), :].astype(jnp.int32).astype(f32)
-            grad[pl.ds(aligned(i * share, 8), share), :] = v * decode(source, base, share)
-
-        each(devices, shares)
+    refs = refs[56:]
+    grads, refs = refs[:count], refs[count:]
+    staged = [refs[3 * i : 3 * i + 3] for i in range(LARGE)]
+    store_sems = refs[3 * LARGE]
 
     def small(row, rows, lanes):
         parts = [g_small[c * SMALL_ROWS + row : c * SMALL_ROWS + row + rows, :] for c in range(lanes // 128)]
         return parts[0] if len(parts) == 1 else jnp.concatenate(parts, axis=1)
-
-    def blocks(member, grad, block_rows, base, count, start=0):
-        size = 64
-
-        def step(i):
-            block = i // (block_rows // size)
-            row = (i % (block_rows // size)) * size
-            here = pl.ds(pl.multiple_of(start + block * block_rows + row, 8), size)
-            columns = members[member][0].shape[1] // 128
-            for c in range(columns):
-                lanes = slice(c * 128, (c + 1) * 128)
-                g = grad[pl.ds(pl.multiple_of(base + (block * columns + c) * block_rows + row, 8), size), :]
-                w, m, v = (ref[here, lanes] for ref in members[member])
-                for out, value in zip(outs[member], adamw(w, g, m, v, rate_matrix)):
-                    out[here, lanes] = value
-
-        each(count * block_rows // size, step)
 
     def single(member, index, grad, rate):
         w, m, v = (ref[index] for ref in members[member])
         for out, value in zip(outs[member], adamw(w, grad, m, v, rate)):
             out[index] = value
 
-    blocks(0, g_pair_a, C1, 0, 9)
-    blocks(0, g_pair_b, C1, 0, 9, 9 * C1)
-    blocks(1, g_down, C1, 0, 9)
-    blocks(2, g_wide, HALF_CHANNELS, 0, 9)
-    blocks(3, g_down, C1, SKIP_ROW, 1)
-    blocks(4, g_attn, HALF_CHANNELS, 0, 1)
+    def unpack(source, grad):
+        share = grad.shape[0] // devices
+
+        def shares(i):
+            base = i * (share + TILE)
+            v = source[pl.ds(aligned(base, TILE), share), :].astype(jnp.int32).astype(f32)
+            grad[pl.ds(aligned(i * share, 8), share), :] = v * decode(source, base, share)
+
+        each(devices, shares)
+
+    def update(part):
+        member, which, block_rows, base, blocks, start = part
+        size = 64
+        grad = grads[which]
+        columns = staged[member][0].shape[1] // 128
+
+        def step(i):
+            block = i // (block_rows // size)
+            row = (i % (block_rows // size)) * size
+            here = pl.ds(aligned(start + block * block_rows + row, 8), size)
+            for c in range(columns):
+                lanes = slice(c * 128, (c + 1) * 128)
+                g = grad[pl.ds(aligned(base + (block * columns + c) * block_rows + row, 8), size), :]
+                w, m, v = (ref[here, lanes] for ref in members[member])
+                for out, value in zip(staged[member], adamw(w, g, m, v, rate_matrix)):
+                    out[here, lanes] = value
+
+        each(blocks * block_rows // size, step)
+
+    stores = []
+    seen = set()
+    for i, part in enumerate(PARTS):
+        member, which, block_rows, _, blocks, start = part
+        if which not in seen:
+            unpack(coded[which], grads[which])
+            seen.add(which)
+        update(part)
+        here = pl.ds(start, block_rows * blocks)
+        for kind in range(3):
+            copy = pltpu.make_async_copy(
+                staged[member][kind].at[here], outs[member][kind].at[here], store_sems.at[i, kind]
+            )
+            copy.start()
+            stores.append(copy)
     for tap in range(9):
         single(5, (tap,), small(tap * 8, 3, HALF_CHANNELS), rate_matrix)
     every = slice(None)
@@ -1271,19 +1308,26 @@
     loss_out[...] = g_small[LOSS_ROW : LOSS_ROW + 1, :]
     diagonal = lax.broadcasted_iota(jnp.int32, (NB, 128), 0) == lax.broadcasted_iota(jnp.int32, (NB, 128), 1)
     counts_out[...] = jnp.sum(jnp.where(diagonal, counts[...], 0.0), axis=0, keepdims=True)[:, :NB]
+    for copy in stores:
+        copy.wait()
 
 
 def update_call(devices, grads, members):
     whole = pl.BlockSpec(memory_space=pltpu.VMEM)
+    outside = pl.BlockSpec(memory_space=pltpu.HBM)
     flat = [v for member in members for v in member]
+    large = [v.shape for v in flat[: 3 * LARGE]]
     return pl.pallas_call(
         functools.partial(update_kernel, devices),
         out_shape=[jax.ShapeDtypeStruct(v.shape, f32) for v in flat]
         + [jax.ShapeDtypeStruct((1, 128), f32), jax.ShapeDtypeStruct((1, NB), f32)],
         in_specs=[whole] * (len(grads) + len(flat)),
-        out_specs=[whole] * (len(flat) + 2),
-        scratch_shapes=[pltpu.VMEM((padded(rows, devices, TILE), 128), f32) for rows in GRADS],
-        compiler_params=pltpu.CompilerParams(vmem_limit_bytes=VMEM_LIMIT),
+        out_specs=[outside] * (3 * LARGE) + [whole] * (len(flat) - 3 * LARGE + 2),
+        scratch_shapes=[pltpu.VMEM((padded(rows, devices, TILE), 128), f32) for rows in GRADS]
+        + [pltpu.VMEM(shape, f32) for shape in large]
+        + [pltpu.SemaphoreType.DMA((len(PARTS), 3))],
+        compiler_params=pltpu.CompilerParams(vmem_limit_bytes=UPDATE_LIMIT),
+        cost_estimate=pl.CostEstimate(flops=30 * 10**6, bytes_accessed=40 * 10**6, transcendentals=0),
     )(*grads, *flat)
 
 
@@ -1365,14 +1409,12 @@
         norm_wide_sq,
         time_bias_sq,
     )
-    masks = halves(pixel_mask)
     summed = main_call(
         dp_size,
         buckets,
         halves(features),
         halves(jnp.transpose(target, (0, 3, 1, 2))),
-        masks,
-        masks,
+        halves(pixel_mask),
         *params,
     )
     results = update_call(2 * dp_size, summed, list(zip(params, firsts, seconds)))

time: 108 us -> 94.8 us (0.88)
  Pallas kernels: 107 us -> 93.2 us
    pallas_call x1, Pallas kernels: 21.8 us -> 10 us  [update_call(): pl.pallas_call(functools.partial(update_kernel, devices), out_shape=[jax....]
    pallas_call x1, Pallas kernels: 85.2 us -> 83.2 us  [main_call(): pl.pallas_call(functools.partial(main_kernel, dp_size), out_shape=[jax.Sh...]
where the time goes in v3:
time: 94.8 us; the launch traced here: 94.6 us
  Pallas kernels  93.2 us (98%)
  between operations  1.27 us (1%)
    pallas_call x1, Pallas kernels, main_call(): pl.pallas_call(functools.partial(main_kernel, dp_size), out_shape=[jax.Sh...  83.2 us
    pallas_call x1, Pallas kernels, update_call(): pl.pallas_call(functools.partial(update_kernel, devices), out_shape=[jax....  10 us

profile of v3, /device:TPU:0, one launch (start us, length us, event | category | flops | bytes accessed | tf_op | source)
XLA Modules:
  0.0 94.6 jit_solution(544068293536865196)
XLA Ops:
  0.7 0.0 copy-start
  0.7 0.0 copy-start.1
  0.7 0.0 copy-start.2
  0.7 0.0 copy-start.3
  0.7 0.0 copy-start.4
  0.7 0.0 copy-start.5
  0.7 0.0 copy-start.6
  0.7 0.0 copy-start.7
  0.8 0.0 copy-start.8
  0.8 0.0 copy-start.9
  0.8 0.0 copy-start.10
  0.8 0.0 copy-start.11
  0.8 0.0 copy-start.12
  0.8 0.0 copy-start.13
  0.8 0.0 copy-start.14
  0.8 0.0 copy-start.15
  0.8 0.0 copy-start.16
  0.8 0.0 copy-start.17
  0.9 0.0 copy-start.18
  0.9 0.0 copy-start.19
  0.9 0.0 copy-start.20
  0.9 0.0 copy-start.21
  0.9 0.0 copy-start.22
  0.9 0.0 copy-start.23
  0.9 0.0 copy-start.24
  0.9 0.0 copy-start.25
  1.0 0.0 copy-start.26
  1.0 83.2 %shard_map.518 = (s16[2560,128]{1,0:T(8,128)(2,1)S(1)}, s16[5120,128]{1,0:T(8,128)(2,1)S(1)}, s16[3072,128]{1,0:T(8,128)(2,1)S(1)}, s16[2048,128]{1,0:T(8,128)(2...) custom-call(s32[4]{0:T(128)} %buckets.1, ...), custom_call_target="tpu_custom_call" | custom-call | flops 8000000000 | bytes 12000000 | tf_op jit(solution)/shard_map/pallas_call | solution.py:914
  84.2 0.0 copy-done
  84.2 0.0 copy-done.1
  84.2 0.0 copy-done.2
  84.2 0.0 copy-done.3
  84.2 0.0 copy-done.4
  84.2 0.0 copy-done.5
  84.3 0.0 copy-done.6
  84.3 0.0 copy-done.7
  84.3 0.0 copy-done.8
  84.3 0.0 copy-done.9
  84.3 0.0 copy-done.10
  84.3 0.0 copy-done.11
  84.3 0.0 copy-done.12
  84.3 0.0 copy-done.13
  84.3 0.0 copy-done.14
  84.3 0.0 copy-done.15
  84.4 0.0 copy-done.16
  84.4 0.0 copy-done.17
  84.4 0.0 copy-done.18
  84.5 10.0 %shard_map.519 = (f32[2304,128]{1,0:T(8,128)}, f32[2304,128]{1,0:T(8,128)}, f32[2304,128]{1,0:T(8,128)}, f32[1152,256]{1,0:T(8,128)}, f32[1152,256]{1,0:T(8,128)...) custom-call(s16[2560,128]{1,0:T(8,128)(2,1)S(1)} %get-tuple-element., ...), custom_call_target="tpu_custom_call" | custom-call | flops 30000000 | bytes 40000000 | tf_op jit(solution)/shard_map/pallas_call | solution.py:1320
  (8 shorter events, 0.0 us)
Async XLA Ops:
  0.7 83.5 %copy-start = (f32[3,3,256,256]{3,2,1,0:T(8,128)S(1)}, f32[3,3,256,256]{3,2,1,0:T(8,128)}, u32[]{:S(2)}) copy-start(f32[3,3,256,256]{3,2,1,0:T(8,128)} %param.37) | copy-start | bytes 7077892
  0.7 83.5 %copy-start.1 = (f32[3,3,256,256]{3,2,1,0:T(8,128)S(1)}, f32[3,3,256,256]{3,2,1,0:T(8,128)}, u32[]{:S(2)}) copy-start(f32[3,3,256,256]{3,2,1,0:T(8,128)} %param.46) | copy-start | bytes 7077892
  0.7 83.5 %copy-start.2 = (f32[3,3,256,256]{3,2,1,0:T(8,128)S(1)}, f32[3,3,256,256]{3,2,1,0:T(8,128)}, u32[]{:S(2)}) copy-start(f32[3,3,256,256]{3,2,1,0:T(8,128)} %param.55) | copy-start | bytes 7077892
  0.7 83.5 %copy-start.3 = (f32[2,3,3,128,128]{4,3,2,1,0:T(8,128)S(1)}, f32[2,3,3,128,128]{4,3,2,1,0:T(8,128)}, u32[]{:S(2)}) copy-start(f32[2,3,3,128,128]{4,3,2,1,0:T(8,128)} %param.35) | copy-start | bytes 3538948
  0.7 83.5 %copy-start.4 = (f32[3,3,128,256]{3,2,1,0:T(8,128)S(1)}, f32[3,3,128,256]{3,2,1,0:T(8,128)}, u32[]{:S(2)}) copy-start(f32[3,3,128,256]{3,2,1,0:T(8,128)} %param.36) | copy-start | bytes 3538948
  0.7 83.5 %copy-start.5 = (f32[2,3,3,128,128]{4,3,2,1,0:T(8,128)S(1)}, f32[2,3,3,128,128]{4,3,2,1,0:T(8,128)}, u32[]{:S(2)}) copy-start(f32[2,3,3,128,128]{4,3,2,1,0:T(8,128)} %param.44) | copy-start | bytes 3538948
  0.7 83.5 %copy-start.6 = (f32[2,3,3,128,128]{4,3,2,1,0:T(8,128)S(1)}, f32[2,3,3,128,128]{4,3,2,1,0:T(8,128)}, u32[]{:S(2)}) copy-start(f32[2,3,3,128,128]{4,3,2,1,0:T(8,128)} %param.53) | copy-start | bytes 3538948
  0.7 83.5 %copy-start.7 = (f32[3,3,128,256]{3,2,1,0:T(8,128)S(1)}, f32[3,3,128,256]{3,2,1,0:T(8,128)}, u32[]{:S(2)}) copy-start(f32[3,3,128,256]{3,2,1,0:T(8,128)} %param.45) | copy-start | bytes 3538948
  0.8 83.5 %copy-start.8 = (f32[3,3,128,256]{3,2,1,0:T(8,128)S(1)}, f32[3,3,128,256]{3,2,1,0:T(8,128)}, u32[]{:S(2)}) copy-start(f32[3,3,128,256]{3,2,1,0:T(8,128)} %param.54) | copy-start | bytes 3538948
  0.8 83.5 %copy-start.9 = (f32[256,1024]{1,0:T(8,128)S(1)}, f32[256,1024]{1,0:T(8,128)}, u32[]{:S(2)}) copy-start(f32[256,1024]{1,0:T(8,128)} %refs_20_.1) | copy-start | bytes 3145732
  0.8 83.5 %copy-start.10 = (f32[256,1024]{1,0:T(8,128)S(1)}, f32[256,1024]{1,0:T(8,128)}, u32[]{:S(2)}) copy-start(f32[256,1024]{1,0:T(8,128)} %refs_21_.1) | copy-start | bytes 3145732
  0.8 83.5 %copy-start.11 = (f32[256,1024]{1,0:T(8,128)S(1)}, f32[256,1024]{1,0:T(8,128)}, u32[]{:S(2)}) copy-start(f32[256,1024]{1,0:T(8,128)} %refs_22_.1) | copy-start | bytes 3145732
  0.8 83.5 %copy-start.12 = (f32[128,256]{1,0:T(8,128)S(1)}, f32[128,256]{1,0:T(8,128)}, u32[]{:S(2)}) copy-start(f32[128,256]{1,0:T(8,128)} %refs_17_.1) | copy-start | bytes 393220
  0.8 83.5 %copy-start.13 = (f32[128,256]{1,0:T(8,128)S(1)}, f32[128,256]{1,0:T(8,128)}, u32[]{:S(2)}) copy-start(f32[128,256]{1,0:T(8,128)} %refs_18_.1) | copy-start | bytes 393220
  0.8 83.5 %copy-start.14 = (f32[128,256]{1,0:T(8,128)S(1)}, f32[128,256]{1,0:T(8,128)}, u32[]{:S(2)}) copy-start(f32[128,256]{1,0:T(8,128)} %refs_19_.1) | copy-start | bytes 393220
  0.8 83.5 %copy-start.15 = (f32[3,3,256,3]{2,3,1,0:T(4,128)S(1)}, f32[3,3,256,3]{2,3,1,0:T(4,128)}, u32[]{:S(2)}) copy-start(f32[3,3,256,3]{2,3,1,0:T(4,128)} %param.40) | copy-start | bytes 82948
  0.8 83.5 %copy-start.16 = (f32[3,3,256,3]{2,3,1,0:T(4,128)S(1)}, f32[3,3,256,3]{2,3,1,0:T(4,128)}, u32[]{:S(2)}) copy-start(f32[3,3,256,3]{2,3,1,0:T(4,128)} %param.49) | copy-start | bytes 82948
  0.8 83.5 %copy-start.17 = (f32[3,3,256,3]{2,3,1,0:T(4,128)S(1)}, f32[3,3,256,3]{2,3,1,0:T(4,128)}, u32[]{:S(2)}) copy-start(f32[3,3,256,3]{2,3,1,0:T(4,128)} %param.58) | copy-start | bytes 82948
  0.9 83.5 %copy-start.18 = (f32[8,384]{1,0:T(8,128)S(1)}, f32[8,384]{1,0:T(8,128)}, u32[]{:S(2)}) copy-start(f32[8,384]{1,0:T(8,128)} %refs_32_.1) | copy-start | bytes 36868
  0.9 83.5 %copy-start.19 = (f32[8,384]{1,0:T(8,128)S(1)}, f32[8,384]{1,0:T(8,128)}, u32[]{:S(2)}) copy-start(f32[8,384]{1,0:T(8,128)} %refs_33_.1) | copy-start | bytes 36868
  0.9 83.5 %copy-start.20 = (f32[8,384]{1,0:T(8,128)S(1)}, f32[8,384]{1,0:T(8,128)}, u32[]{:S(2)}) copy-start(f32[8,384]{1,0:T(8,128)} %refs_34_.1) | copy-start | bytes 36868
  0.9 83.5 %copy-start.21 = (f32[6,256]{1,0:T(8,128)S(1)}, f32[6,256]{1,0:T(8,128)}, u32[]{:S(2)}) copy-start(f32[6,256]{1,0:T(8,128)} %refs_29_.1) | copy-start | bytes 18436
  0.9 83.5 %copy-start.22 = (f32[6,256]{1,0:T(8,128)S(1)}, f32[6,256]{1,0:T(8,128)}, u32[]{:S(2)}) copy-start(f32[6,256]{1,0:T(8,128)} %refs_30_.1) | copy-start | bytes 18436
  0.9 83.5 %copy-start.23 = (f32[6,256]{1,0:T(8,128)S(1)}, f32[6,256]{1,0:T(8,128)}, u32[]{:S(2)}) copy-start(f32[6,256]{1,0:T(8,128)} %refs_31_.1) | copy-start | bytes 18436
  0.9 83.5 %copy-start.24 = (f32[6,128]{1,0:T(8,128)S(1)}, f32[6,128]{1,0:T(8,128)}, u32[]{:S(2)}) copy-start(f32[6,128]{1,0:T(8,128)} %refs_26_.1) | copy-start | bytes 9220
  0.9 83.5 %copy-start.25 = (f32[6,128]{1,0:T(8,128)S(1)}, f32[6,128]{1,0:T(8,128)}, u32[]{:S(2)}) copy-start(f32[6,128]{1,0:T(8,128)} %refs_27_.1) | copy-start | bytes 9220
  1.0 83.5 %copy-start.26 = (f32[6,128]{1,0:T(8,128)S(1)}, f32[6,128]{1,0:T(8,128)}, u32[]{:S(2)}) copy-start(f32[6,128]{1,0:T(8,128)} %refs_28_.1) | copy-start | bytes 9220

commit v4 on v3

--- a/solution.py
+++ b/solution.py
@@ -282,6 +282,7 @@
     x_in, target, mask, down, wide, skip, attn, head, gains_narrow, gains_wide, time_bias, mask_local,
     g_attn, g_wide, g_down, g_pair_b, g_pair_a, g_rows,
     out_attn, out_wide, out_down, out_pair_b, out_pair_a,
+    half_attn, half_wide, half_down, half_pair_b, half_pair_a,
     in_attn, in_wide, in_down, in_pair_b, in_pair_a, in_small,
     sems_attn, sems_wide, sems_down, sems_pair_b, sems_pair_a, sems_small,
     g_small, g_late,
@@ -358,11 +359,12 @@
     counting.step()
     sources = (g_attn, g_wide, g_down, g_pair_b, g_pair_a, g_rows)
     outgoing = (out_attn, out_wide, out_down, out_pair_b, out_pair_a, None)
+    halves = (half_attn, half_wide, half_down, half_pair_b, half_pair_a, None)
     incoming = (in_attn, in_wide, in_down, in_pair_b, in_pair_a, in_small)
     outs = (sum_attn, sum_wide, sum_down, sum_pair_b, sum_pair_a, sum_small)
     sems = (sems_attn, sems_wide, sems_down, sems_pair_b, sems_pair_a, sems_small)
-    orders = (links.brief, links.full, links.brief, links.brief, links.brief, links.brief)
-    pieces = dict(zip(PIECE_NAMES, (Piece(*parts) for parts in zip(sources, outgoing, incoming, outs, sems, orders))))
+    orders = (links.brief, links.brief, links.brief, links.brief, links.brief, links.brief)
+    pieces = dict(zip(PIECE_NAMES, (Piece(*parts) for parts in zip(sources, outgoing, halves, incoming, outs, sems, orders))))
 
     def advance(point):
         for name in SCHEDULE.get(point, ()):
@@ -652,6 +654,7 @@
         g_small[WIDE_NORM_ROW + 3 : WIDE_NORM_ROW + 4, :] += shift[0:1, :]
         grad = dy * ca[0:1, :] + v * cb[0:1, :] + cd[0:1, :] + dwide[n] * root_half
         store_shifted(cells_g, n, 0, (grad * root_half).reshape(HALF, HALF, HALF_CHANNELS))
+        advance("gn_e%d" % n)
 
     center = cells_g[:, 1, 1 : HALF + 1].reshape(-1, HALF_CHANNELS)
     for dy in range(3):
@@ -682,6 +685,7 @@
         grad = dy * ca[0:1, :] + v * cb[0:1, :] + cd[0:1, :]
         time_wide = time_wide + jnp.where(bucket_rows == bucket(n), total(fold(grad)), 0.0)
         store_shifted(cells_g, n, 0, grad.reshape(HALF, HALF, HALF_CHANNELS))
+        advance("gn_d%d" % n)
     g_small[TIME_WIDE_ROW : TIME_WIDE_ROW + NB, :] = time_wide
 
     for c in range(2):
@@ -731,13 +735,18 @@
                 sum_dyv = sum_dyv + fold(dy * v)
             return sum_dy, sum_dyv
 
-        sum_dy, sum_dyv = lax.fori_loop(0, 4, step, (zero_n, zero_n))
+        carry = (zero_n, zero_n)
+        for part in range(2):
+            carry = lax.fori_loop(2 * part, 2 * part + 2, step, carry)
+            if part == 0:
+                advance("t%da0" % n)
+        sum_dy, sum_dyv = carry
         gain, shift, ca, cb, cd = norm_grad_coefs(
             sum_dy, sum_dyv, gain_n(4), coef_n[2, n, 2], coef_n[2, n, 3], full_pixels
         )
         g_late[4:5, :] += gain[0:1, :]
         g_late[5:6, :] += shift[0:1, :]
-        advance("t%da" % n)
+        advance("t%da1" % n)
 
         def finish(i):
             parts = up_parts(dfs, n, i, size)
@@ -748,12 +757,13 @@
                 g = g + dy_full[n, b, here] * ca[0:1, :] + v * cb[0:1, :] + cd[0:1, :]
                 store_planes(in_g, n, b, i * 2 * size, rounded(g) * root_half)
 
-        each(4, finish)
+        for part in range(2):
+            each(2, lambda i: finish(2 * part + i))
+            advance("t%db%d" % (n, part))
 
     advance("narrow")
     for n in range(images):
         third_norm(n)
-        advance("t%db" % n)
 
     def pair_gradient(planes, member):
         products = None
@@ -777,7 +787,7 @@
             out = mm_nt(pair_input(in_g, b, range(4)), pair_bwd[member])
             for n in range(images):
                 dy_full[n, b, pl.ds(0, RES)] = pair_rows(out, n)
-        advance("b%dc" % member)
+            advance("b%dc" % member if b else "b%dc0" % member)
         bucket_rows = lax.broadcasted_iota(jnp.int32, (NB, C1), 0)
 
         def image(n):
@@ -804,6 +814,7 @@
             g_late[gain_row + 1 : gain_row + 2, :] += shift[0:1, :]
             if last:
                 return
+            advance("b%di%da" % (member, n))
 
             def finish(i, carry):
                 here = pl.ds(i * ROWS, ROWS)
@@ -842,11 +853,12 @@
     n = operands[1].shape[1]
     devices = 2 * dp_size
     counts = group_sizes(dp_size)
-    orders = (counts[1], counts[0]) + (counts[1],) * 4
+    orders = (counts[1], counts[1], counts[1], counts[1], counts[1], counts[1])
     grads = [padded(rows, devices, TILE) for rows in GRADS]
     sums = [(coded_rows(rows, devices), jnp.int16) for rows in GRADS]
     sums.append((padded(2 * SMALL_ROWS, devices, 8), f32))
-    spaces = [message_rows(rows, order, TILE) for rows, order in zip(grads, orders)]
+    spaces = [message_rows(rows // 2, order[1:], TILE) for rows, order in zip(grads, orders)]
+    sent = [message_rows(rows // 2, order[1:], TILE, 1) for rows, order in zip(grads, orders)]
     small_space = message_rows(sums[-1][0], orders[-1], 0)
     stages = sum(size - 1 for size in counts[1])
     vm = pltpu.VMEM
@@ -856,7 +868,8 @@
     square = (n, HALF * HALF, wide)
     moved = [vm(v.shape, v.dtype) for v in operands[1:4] + operands[5:] + operands[3:4]]
     scratch = moved + [vm((rows, 128), f32) for rows in grads + [sums[-1][0]]]
-    scratch += [vm((rows, 128), jnp.int16) for rows in spaces]
+    scratch += [vm((rows, 128), jnp.int16) for rows in sent]
+    scratch += [vm((rows // 2, 128), f32) for rows in grads]
     scratch += [vm((rows, 128), jnp.int16) for rows in spaces] + [vm((small_space, 128), f32)]
     scratch += [pltpu.SemaphoreType.DMA((2, 2 * sum(size - 1 for size in order))) for order in orders]
     scratch += [
@@ -927,19 +940,23 @@
 PIECE_NAMES = ("attn", "wide", "down", "pair_b", "pair_a", "small")
 SCHEDULE = {
     "attn": ("attn",),
-    "wide": ("wide", "attn"),
-    "gn_d": ("small", "wide"),
-    "down": ("down", "small"),
-    "t0a": ("down", "attn"),
-    "t1a": ("wide",),
-    "t1b": ("small",),
-    "pair_b": ("pair_b",),
-    "b1c": ("attn",),
-    "b1i0": ("pair_b", "down", "small", "wide"),
-    "pair_a": ("pair_a",),
-    "b0c": ("attn",),
-    "b0i0": ("pair_a", "pair_b"),
-    "end": ("late", "down", "small", "late", "wide", "attn", "pair_b", "attn", "pair_a", "down", "small", "late", "small", "wide", "pair_b", "pair_a", "down", "late", "wide", "down", "pair_a", "pair_b", "pair_b", "wide", "wide", "pair_a", "pair_a"),
+    "wide": ("wide",),
+    "conv_d": ("attn",),
+    "gn_d": ("small",),
+    "down": ("down",),
+    "t0a0": ("wide", "small",),
+    "t0a1": ("down", "attn",),
+    "pair_b": ("pair_b", "attn",),
+    "b1i0a": ("wide", "small", "pair_b",),
+    "b1i1a": ("attn",),
+    "pair_a": ("pair_a", "down",),
+    "b0c": ("wide", "small", "pair_b", "pair_a",),
+    "end": (
+        "late", "down", "attn", "late", "pair_a", "wide", "attn", "small",
+        "pair_b", "late", "down", "pair_a", "pair_b", "late", "wide", "small",
+        "pair_a", "wide", "small", "down", "down", "pair_b", "pair_b", "pair_a",
+        "pair_a",
+    ),
 }
 
 
@@ -950,7 +967,7 @@
     while k < bits:
         far.append(1 << min(2, bits - k))
         k += 2
-    return [2, 2, 2] + far, [2, 4] + far
+    return [2, 2, 2] + far, [2, 4] + far, [2] + far + [4]
 
 
 class Links:
@@ -983,6 +1000,7 @@
             unit *= size
         self.full = [along(1, 2), second, third] + far
         self.brief = [along(1, 2), (place, square)] + far
+        self.far_first = [along(1, 2)] + far + [(place, square)]
         self.all = [other for _, others in self.brief for other in others]
 
     def greet(self):
@@ -1063,8 +1081,10 @@
     return row if isinstance(row, int) else pl.multiple_of(row, tile)
 
 
-def encode(source, first, rows, target, base):
-    size = chunk_of(rows)
+def encode(source, first, rows, parts, target, base):
+    part = rows // parts
+    size = chunk_of(part)
+    per_part = part // size
 
     def largest(i, carry):
         v = jnp.abs(source[pl.ds(aligned(first + i * size, 8), size), :])
@@ -1077,13 +1097,14 @@
 
     def step(i):
         v = source[pl.ds(aligned(first + i * size, 8), size), :] * scale
-        v = jnp.clip(jnp.round(v), -32767.0, 32767.0)
-        target[pl.ds(aligned(base + i * size, TILE), size), :] = v.astype(jnp.int32).astype(jnp.int16)
+        v = jnp.clip(jnp.round(v), -32767.0, 32767.0).astype(jnp.int32).astype(jnp.int16)
+        row = base + i * size + (i // per_part) * TILE
+        target[pl.ds(aligned(row, TILE), size), :] = v
 
     each(rows // size, step)
-    target[pl.ds(aligned(base + rows, TILE), TILE), :] = jnp.broadcast_to(
-        power.astype(jnp.int32), (TILE, 128)
-    ).astype(jnp.int16)
+    tile = jnp.broadcast_to(power.astype(jnp.int32), (TILE, 128)).astype(jnp.int16)
+    for m in range(parts):
+        target[pl.ds(aligned(base + m * (part + TILE) + part, TILE), TILE), :] = tile
 
 
 def decode(source, base, rows):
@@ -1091,22 +1112,23 @@
     return jnp.exp2(power[0:1, :] - 15.0)
 
 
-def message_rows(rows, sizes, tile):
+def message_rows(rows, sizes, tile, own=0):
     needed = 0
     for size in sizes:
         rows //= size
-        needed += (size - 1) * (rows + tile)
+        needed += (size - 1 + (own if size > 2 else 0)) * (rows + tile)
     return needed
 
 
 class Piece:
-    def __init__(self, source, outgoing, arrived, out, sems, stages):
-        self.source, self.outgoing, self.arrived, self.out, self.sems = source, outgoing, arrived, out, sems
+    def __init__(self, source, outgoing, half, arrived, out, sems, stages):
+        self.source, self.outgoing, self.half, self.arrived = source, outgoing, half, arrived
+        self.out, self.sems = out, sems
         self.stages = stages
         self.tile = 0 if outgoing is None else TILE
         self.rows = source.shape[0]
         self.first = 0
-        self.base = self.index = self.t = 0
+        self.base = self.sent = self.index = self.t = 0
         self.copies = []
         self.share = self.rows
         for _, others in stages:
@@ -1133,19 +1155,26 @@
         place, others = stage
         size = len(others) + 1
         rows = self.rows // size
-        block = rows + self.tile
+        raw = self.half is not None and self.t == 0
+        tile = 0 if raw else self.tile
+        block = rows + tile
+        arrived = self.half if raw else self.arrived
+        if tile and size > 2:
+            encode(self.source, self.first, self.rows, size, self.outgoing, self.sent)
         for r, other in enumerate(others):
-            part = self.first + ((place + r + 1) % size) * rows
-            if self.tile:
-                mine = self.base + r * block
-                encode(self.source, part, rows, self.outgoing, mine)
-                message = self.outgoing.at[pl.ds(mine, block)]
+            member = (place + r + 1) % size
+            part = self.first + member * rows
+            if tile and size > 2:
+                message = self.outgoing.at[pl.ds(aligned(self.sent + member * block, TILE), block)]
+            elif tile:
+                encode(self.source, part, rows, 1, self.outgoing, self.sent)
+                message = self.outgoing.at[pl.ds(self.sent, block)]
             else:
                 message = self.source.at[pl.ds(aligned(part, 8), rows)]
             landing = size - 2 - r
             copy = send(
                 message,
-                self.arrived.at[pl.ds(self.base + landing * block, block)],
+                arrived.at[pl.ds(self.base + landing * block, block)],
                 self.sems,
                 self.index + r,
                 self.index + landing,
@@ -1158,24 +1187,29 @@
         place, others = stage
         size = len(others) + 1
         rows = self.rows // size
-        block = rows + self.tile
+        raw = self.half is not None and self.t == 1
+        tile = 0 if raw else self.tile
+        block = rows + tile
+        arrived = self.half if raw else self.arrived
         for copy in self.copies:
             copy.wait()
         first = self.first + place * rows
-        scales = [decode(self.arrived, self.base + r * block, rows) if self.tile else 1.0 for r in range(size - 1)]
+        scales = [decode(arrived, self.base + r * block, rows) if tile else 1.0 for r in range(size - 1)]
         chunk = chunk_of(rows)
 
         def add(i):
             here = pl.ds(aligned(first + i * chunk, 8), chunk)
             v = self.source[here, :]
             for r, scale in enumerate(scales):
-                more = self.arrived[pl.ds(aligned(self.base + r * block + i * chunk, self.tile or 8), chunk), :]
-                v = v + (more.astype(jnp.int32).astype(f32) * scale if self.tile else more)
+                more = arrived[pl.ds(aligned(self.base + r * block + i * chunk, tile or 8), chunk), :]
+                v = v + (more.astype(jnp.int32).astype(f32) * scale if tile else more)
             self.source[here, :] = v
 
         each(rows // chunk, add)
         self.first, self.rows = first, rows
-        self.base += (size - 1) * block
+        if not raw:
+            self.base += (size - 1) * block
+            self.sent += (size if size > 2 else 1) * block
         self.index += size - 1
         self.copies = []
 
@@ -1187,7 +1221,7 @@
         self.first = self.place * block
         self.rows = block
         if self.tile:
-            encode(self.source, self.place * self.share, self.share, self.out, self.first)
+            encode(self.source, self.place * self.share, self.share, 1, self.out, self.first)
         else:
             self.out[pl.ds(aligned(self.first, 8), block), :] = self.source[
                 pl.ds(aligned(self.first, 8), block), :

time: 94.8 us -> 91.7 us (0.967)
  Pallas kernels: 93.2 us -> 90.2 us
    pallas_call x1, Pallas kernels: 83.2 us -> 80.2 us  [main_call(): pl.pallas_call(functools.partial(main_kernel, dp_size), out_shape=[jax.Sh...]
where the time goes in v4:
time: 91.7 us; the launch traced here: 91.6 us
  Pallas kernels  90.2 us (98%)
  between operations  1.27 us (1%)
    pallas_call x1, Pallas kernels, main_call(): pl.pallas_call(functools.partial(main_kernel, dp_size), out_shape=[jax.Sh...  80.2 us
    pallas_call x1, Pallas kernels, update_call(): pl.pallas_call(functools.partial(update_kernel, devices), out_shape=[jax....  10 us

profile of v4, /device:TPU:0, one launch (start us, length us, event | category | flops | bytes accessed | tf_op | source)
XLA Modules:
  0.0 91.6 jit_solution(17502885976905178567)
XLA Ops:
  0.7 0.0 copy-start
  0.7 0.0 copy-start.1
  0.7 0.0 copy-start.2
  0.7 0.0 copy-start.3
  0.7 0.0 copy-start.4
  0.7 0.0 copy-start.5
  0.7 0.0 copy-start.6
  0.7 0.0 copy-start.7
  0.8 0.0 copy-start.8
  0.8 0.0 copy-start.9
  0.8 0.0 copy-start.10
  0.8 0.0 copy-start.11
  0.9 0.0 copy-start.20
  0.9 0.0 copy-start.21
  0.9 0.0 copy-start.22
  0.9 0.0 copy-start.23
  0.9 0.0 copy-start.24
  0.9 0.0 copy-start.25
  1.0 0.0 copy-start.26
  1.0 80.2 %shard_map.518 = (s16[2560,128]{1,0:T(8,128)(2,1)S(1)}, s16[5120,128]{1,0:T(8,128)(2,1)S(1)}, s16[3072,128]{1,0:T(8,128)(2,1)S(1)}, s16[2048,128]{1,0:T(8,128)(2...) custom-call(s32[4]{0:T(128)} %buckets.1, ...), custom_call_target="tpu_custom_call" | custom-call | flops 8000000000 | bytes 12000000 | tf_op jit(solution)/shard_map/pallas_call | solution.py:927
  81.1 0.0 copy-done
  81.1 0.0 copy-done.1
  81.2 0.0 copy-done.2
  81.2 0.0 copy-done.3
  81.2 0.0 copy-done.4
  81.2 0.0 copy-done.5
  81.2 0.0 copy-done.6
  81.2 0.0 copy-done.7
  81.2 0.0 copy-done.8
  81.2 0.0 copy-done.9
  81.2 0.0 copy-done.10
  81.2 0.0 copy-done.11
  81.3 0.0 copy-done.12
  81.3 0.0 copy-done.13
  81.3 0.0 copy-done.14
  81.3 0.0 copy-done.15
  81.3 0.0 copy-done.16
  81.3 0.0 copy-done.17
  81.3 0.0 copy-done.18
  81.3 0.0 copy-done.19
  81.3 0.0 copy-done.20
  81.3 0.0 copy-done.21
  81.4 0.0 copy-done.22
  81.4 0.0 copy-done.23
  81.4 0.0 copy-done.24
  81.4 0.0 copy-done.25
  81.4 0.0 copy-done.26
  81.4 10.0 %shard_map.519 = (f32[2304,128]{1,0:T(8,128)}, f32[2304,128]{1,0:T(8,128)}, f32[2304,128]{1,0:T(8,128)}, f32[1152,256]{1,0:T(8,128)}, f32[1152,256]{1,0:T(8,128)...) custom-call(s16[2560,128]{1,0:T(8,128)(2,1)S(1)} %get-tuple-element., ...), custom_call_target="tpu_custom_call" | custom-call | flops 30000000 | bytes 40000000 | tf_op jit(solution)/shard_map/pallas_call | solution.py:1354
  (8 shorter events, 0.0 us)
Async XLA Ops:
  0.7 80.5 %copy-start = (f32[3,3,256,256]{3,2,1,0:T(8,128)S(1)}, f32[3,3,256,256]{3,2,1,0:T(8,128)}, u32[]{:S(2)}) copy-start(f32[3,3,256,256]{3,2,1,0:T(8,128)} %param.37) | copy-start | bytes 7077892
  0.7 80.5 %copy-start.1 = (f32[3,3,256,256]{3,2,1,0:T(8,128)S(1)}, f32[3,3,256,256]{3,2,1,0:T(8,128)}, u32[]{:S(2)}) copy-start(f32[3,3,256,256]{3,2,1,0:T(8,128)} %param.46) | copy-start | bytes 7077892
  0.7 80.5 %copy-start.2 = (f32[3,3,256,256]{3,2,1,0:T(8,128)S(1)}, f32[3,3,256,256]{3,2,1,0:T(8,128)}, u32[]{:S(2)}) copy-start(f32[3,3,256,256]{3,2,1,0:T(8,128)} %param.55) | copy-start | bytes 7077892
  0.7 80.5 %copy-start.3 = (f32[2,3,3,128,128]{4,3,2,1,0:T(8,128)S(1)}, f32[2,3,3,128,128]{4,3,2,1,0:T(8,128)}, u32[]{:S(2)}) copy-start(f32[2,3,3,128,128]{4,3,2,1,0:T(8,128)} %param.35) | copy-start | bytes 3538948
  0.7 80.5 %copy-start.4 = (f32[3,3,128,256]{3,2,1,0:T(8,128)S(1)}, f32[3,3,128,256]{3,2,1,0:T(8,128)}, u32[]{:S(2)}) copy-start(f32[3,3,128,256]{3,2,1,0:T(8,128)} %param.36) | copy-start | bytes 3538948
  0.7 80.5 %copy-start.5 = (f32[2,3,3,128,128]{4,3,2,1,0:T(8,128)S(1)}, f32[2,3,3,128,128]{4,3,2,1,0:T(8,128)}, u32[]{:S(2)}) copy-start(f32[2,3,3,128,128]{4,3,2,1,0:T(8,128)} %param.44) | copy-start | bytes 3538948
  0.7 80.5 %copy-start.6 = (f32[2,3,3,128,128]{4,3,2,1,0:T(8,128)S(1)}, f32[2,3,3,128,128]{4,3,2,1,0:T(8,128)}, u32[]{:S(2)}) copy-start(f32[2,3,3,128,128]{4,3,2,1,0:T(8,128)} %param.53) | copy-start | bytes 3538948
  0.7 80.5 %copy-start.7 = (f32[3,3,128,256]{3,2,1,0:T(8,128)S(1)}, f32[3,3,128,256]{3,2,1,0:T(8,128)}, u32[]{:S(2)}) copy-start(f32[3,3,128,256]{3,2,1,0:T(8,128)} %param.45) | copy-start | bytes 3538948
  0.8 80.5 %copy-start.8 = (f32[3,3,128,256]{3,2,1,0:T(8,128)S(1)}, f32[3,3,128,256]{3,2,1,0:T(8,128)}, u32[]{:S(2)}) copy-start(f32[3,3,128,256]{3,2,1,0:T(8,128)} %param.54) | copy-start | bytes 3538948
  0.8 80.5 %copy-start.9 = (f32[256,1024]{1,0:T(8,128)S(1)}, f32[256,1024]{1,0:T(8,128)}, u32[]{:S(2)}) copy-start(f32[256,1024]{1,0:T(8,128)} %refs_20_.1) | copy-start | bytes 3145732
  0.8 80.5 %copy-start.10 = (f32[256,1024]{1,0:T(8,128)S(1)}, f32[256,1024]{1,0:T(8,128)}, u32[]{:S(2)}) copy-start(f32[256,1024]{1,0:T(8,128)} %refs_21_.1) | copy-start | bytes 3145732
  0.8 80.5 %copy-start.11 = (f32[256,1024]{1,0:T(8,128)S(1)}, f32[256,1024]{1,0:T(8,128)}, u32[]{:S(2)}) copy-start(f32[256,1024]{1,0:T(8,128)} %refs_22_.1) | copy-start | bytes 3145732
  0.8 80.5 %copy-start.12 = (f32[128,256]{1,0:T(8,128)S(1)}, f32[128,256]{1,0:T(8,128)}, u32[]{:S(2)}) copy-start(f32[128,256]{1,0:T(8,128)} %refs_17_.1) | copy-start | bytes 393220
  0.8 80.5 %copy-start.13 = (f32[128,256]{1,0:T(8,128)S(1)}, f32[128,256]{1,0:T(8,128)}, u32[]{:S(2)}) copy-start(f32[128,256]{1,0:T(8,128)} %refs_18_.1) | copy-start | bytes 393220
  0.8 80.5 %copy-start.14 = (f32[128,256]{1,0:T(8,128)S(1)}, f32[128,256]{1,0:T(8,128)}, u32[]{:S(2)}) copy-start(f32[128,256]{1,0:T(8,128)} %refs_19_.1) | copy-start | bytes 393220
  0.8 80.5 %copy-start.15 = (f32[3,3,256,3]{2,3,1,0:T(4,128)S(1)}, f32[3,3,256,3]{2,3,1,0:T(4,128)}, u32[]{:S(2)}) copy-start(f32[3,3,256,3]{2,3,1,0:T(4,128)} %param.40) | copy-start | bytes 82948
  0.8 80.5 %copy-start.16 = (f32[3,3,256,3]{2,3,1,0:T(4,128)S(1)}, f32[3,3,256,3]{2,3,1,0:T(4,128)}, u32[]{:S(2)}) copy-start(f32[3,3,256,3]{2,3,1,0:T(4,128)} %param.49) | copy-start | bytes 82948
  0.8 80.5 %copy-start.17 = (f32[3,3,256,3]{2,3,1,0:T(4,128)S(1)}, f32[3,3,256,3]{2,3,1,0:T(4,128)}, u32[]{:S(2)}) copy-start(f32[3,3,256,3]{2,3,1,0:T(4,128)} %param.58) | copy-start | bytes 82948
  0.9 80.5 %copy-start.18 = (f32[8,384]{1,0:T(8,128)S(1)}, f32[8,384]{1,0:T(8,128)}, u32[]{:S(2)}) copy-start(f32[8,384]{1,0:T(8,128)} %refs_32_.1) | copy-start | bytes 36868
  0.9 80.5 %copy-start.19 = (f32[8,384]{1,0:T(8,128)S(1)}, f32[8,384]{1,0:T(8,128)}, u32[]{:S(2)}) copy-start(f32[8,384]{1,0:T(8,128)} %refs_33_.1) | copy-start | bytes 36868
  0.9 80.5 %copy-start.20 = (f32[8,384]{1,0:T(8,128)S(1)}, f32[8,384]{1,0:T(8,128)}, u32[]{:S(2)}) copy-start(f32[8,384]{1,0:T(8,128)} %refs_34_.1) | copy-start | bytes 36868
  0.9 80.5 %copy-start.21 = (f32[6,256]{1,0:T(8,128)S(1)}, f32[6,256]{1,0:T(8,128)}, u32[]{:S(2)}) copy-start(f32[6,256]{1,0:T(8,128)} %refs_29_.1) | copy-start | bytes 18436
  0.9 80.5 %copy-start.22 = (f32[6,256]{1,0:T(8,128)S(1)}, f32[6,256]{1,0:T(8,128)}, u32[]{:S(2)}) copy-start(f32[6,256]{1,0:T(8,128)} %refs_30_.1) | copy-start | bytes 18436
  0.9 80.5 %copy-start.23 = (f32[6,256]{1,0:T(8,128)S(1)}, f32[6,256]{1,0:T(8,128)}, u32[]{:S(2)}) copy-start(f32[6,256]{1,0:T(8,128)} %refs_31_.1) | copy-start | bytes 18436
  0.9 80.5 %copy-start.24 = (f32[6,128]{1,0:T(8,128)S(1)}, f32[6,128]{1,0:T(8,128)}, u32[]{:S(2)}) copy-start(f32[6,128]{1,0:T(8,128)} %refs_26_.1) | copy-start | bytes 9220
  0.9 80.4 %copy-start.25 = (f32[6,128]{1,0:T(8,128)S(1)}, f32[6,128]{1,0:T(8,128)}, u32[]{:S(2)}) copy-start(f32[6,128]{1,0:T(8,128)} %refs_27_.1) | copy-start | bytes 9220
  1.0 80.4 %copy-start.26 = (f32[6,128]{1,0:T(8,128)S(1)}, f32[6,128]{1,0:T(8,128)}, u32[]{:S(2)}) copy-start(f32[6,128]{1,0:T(8,128)} %refs_28_.1) | copy-start | bytes 9220

commit v5 on v4

--- a/solution.py
+++ b/solution.py
@@ -146,12 +146,12 @@
     )
 
 
-def each(count, body):
+def each(count, body, unroll=1):
     def step(i, carry):
         body(i)
         return carry
 
-    lax.fori_loop(0, count, step, 0)
+    lax.fori_loop(0, count, step, 0, unroll=unroll)
 
 
 def prepare_weights(pair, down, wide, skip, attn, head, pair_fwd, pair_bwd, down_fwd, down_bwd, wide_fwd, wide_bwd, skip_low, attn_low, head_low):
@@ -1296,11 +1296,11 @@
             v = source[pl.ds(aligned(base, TILE), share), :].astype(jnp.int32).astype(f32)
             grad[pl.ds(aligned(i * share, 8), share), :] = v * decode(source, base, share)
 
-        each(devices, shares)
+        each(devices, shares, 4)
 
     def update(part):
         member, which, block_rows, base, blocks, start = part
-        size = 64
+        size = 128
         grad = grads[which]
         columns = staged[member][0].shape[1] // 128
 

time: 91.7 us -> 89.7 us (0.978)
  Pallas kernels: 90.2 us -> 88.1 us
    pallas_call x1, Pallas kernels: 10 us -> 7.97 us  [update_call(): pl.pallas_call(functools.partial(update_kernel, devices), out_shape=[jax....]
where the time goes in v5:
time: 89.7 us; the launch traced here: 89.5 us
  Pallas kernels  88.1 us (98%)
  between operations  1.27 us (1%)
    pallas_call x1, Pallas kernels, main_call(): pl.pallas_call(functools.partial(main_kernel, dp_size), out_shape=[jax.Sh...  80.2 us
    pallas_call x1, Pallas kernels, update_call(): pl.pallas_call(functools.partial(update_kernel, devices), out_shape=[jax....  7.97 us

profile of v5, /device:TPU:0, one launch (start us, length us, event | category | flops | bytes accessed | tf_op | source)
XLA Modules:
  0.0 89.5 jit_solution(14802789165175707029)
XLA Ops:
  0.7 0.0 copy-start
  0.7 0.0 copy-start.1
  0.7 0.0 copy-start.2
  0.7 0.0 copy-start.3
  0.7 0.0 copy-start.4
  0.7 0.0 copy-start.5
  0.7 0.0 copy-start.6
  0.7 0.0 copy-start.7
  0.8 0.0 copy-start.8
  0.8 0.0 copy-start.9
  0.8 0.0 copy-start.10
  0.8 0.0 copy-start.11
  0.9 0.0 copy-start.20
  0.9 0.0 copy-start.21
  0.9 0.0 copy-start.22
  0.9 0.0 copy-start.23
  0.9 0.0 copy-start.24
  0.9 0.0 copy-start.25
  1.0 0.0 copy-start.26
  1.0 80.2 %shard_map.518 = (s16[2560,128]{1,0:T(8,128)(2,1)S(1)}, s16[5120,128]{1,0:T(8,128)(2,1)S(1)}, s16[3072,128]{1,0:T(8,128)(2,1)S(1)}, s16[2048,128]{1,0:T(8,128)(2...) custom-call(s32[4]{0:T(128)} %buckets.1, ...), custom_call_target="tpu_custom_call" | custom-call | flops 8000000000 | bytes 12000000 | tf_op jit(solution)/shard_map/pallas_call | solution.py:927
  81.1 0.0 copy-done
  81.1 0.0 copy-done.1
  81.2 0.0 copy-done.2
  81.2 0.0 copy-done.3
  81.2 0.0 copy-done.4
  81.2 0.0 copy-done.5
  81.2 0.0 copy-done.6
  81.2 0.0 copy-done.7
  81.2 0.0 copy-done.8
  81.2 0.0 copy-done.9
  81.2 0.0 copy-done.10
  81.2 0.0 copy-done.11
  81.3 0.0 copy-done.12
  81.3 0.0 copy-done.13
  81.3 0.0 copy-done.14
  81.3 0.0 copy-done.15
  81.3 0.0 copy-done.16
  81.3 0.0 copy-done.17
  81.3 0.0 copy-done.18
  81.3 0.0 copy-done.19
  81.3 0.0 copy-done.20
  81.3 0.0 copy-done.21
  81.4 0.0 copy-done.22
  81.4 0.0 copy-done.23
  81.4 0.0 copy-done.24
  81.4 0.0 copy-done.25
  81.4 0.0 copy-done.26
  81.4 8.0 %shard_map.519 = (f32[2304,128]{1,0:T(8,128)}, f32[2304,128]{1,0:T(8,128)}, f32[2304,128]{1,0:T(8,128)}, f32[1152,256]{1,0:T(8,128)}, f32[1152,256]{1,0:T(8,128)...) custom-call(s16[2560,128]{1,0:T(8,128)(2,1)S(1)} %get-tuple-element., ...), custom_call_target="tpu_custom_call" | custom-call | flops 30000000 | bytes 40000000 | tf_op jit(solution)/shard_map/pallas_call | solution.py:1354
  (8 shorter events, 0.0 us)
Async XLA Ops:
  0.7 80.5 %copy-start = (f32[3,3,256,256]{3,2,1,0:T(8,128)S(1)}, f32[3,3,256,256]{3,2,1,0:T(8,128)}, u32[]{:S(2)}) copy-start(f32[3,3,256,256]{3,2,1,0:T(8,128)} %param.37) | copy-start | bytes 7077892
  0.7 80.5 %copy-start.1 = (f32[3,3,256,256]{3,2,1,0:T(8,128)S(1)}, f32[3,3,256,256]{3,2,1,0:T(8,128)}, u32[]{:S(2)}) copy-start(f32[3,3,256,256]{3,2,1,0:T(8,128)} %param.46) | copy-start | bytes 7077892
  0.7 80.5 %copy-start.2 = (f32[3,3,256,256]{3,2,1,0:T(8,128)S(1)}, f32[3,3,256,256]{3,2,1,0:T(8,128)}, u32[]{:S(2)}) copy-start(f32[3,3,256,256]{3,2,1,0:T(8,128)} %param.55) | copy-start | bytes 7077892
  0.7 80.5 %copy-start.3 = (f32[2,3,3,128,128]{4,3,2,1,0:T(8,128)S(1)}, f32[2,3,3,128,128]{4,3,2,1,0:T(8,128)}, u32[]{:S(2)}) copy-start(f32[2,3,3,128,128]{4,3,2,1,0:T(8,128)} %param.35) | copy-start | bytes 3538948
  0.7 80.5 %copy-start.4 = (f32[3,3,128,256]{3,2,1,0:T(8,128)S(1)}, f32[3,3,128,256]{3,2,1,0:T(8,128)}, u32[]{:S(2)}) copy-start(f32[3,3,128,256]{3,2,1,0:T(8,128)} %param.36) | copy-start | bytes 3538948
  0.7 80.5 %copy-start.5 = (f32[2,3,3,128,128]{4,3,2,1,0:T(8,128)S(1)}, f32[2,3,3,128,128]{4,3,2,1,0:T(8,128)}, u32[]{:S(2)}) copy-start(f32[2,3,3,128,128]{4,3,2,1,0:T(8,128)} %param.44) | copy-start | bytes 3538948
  0.7 80.5 %copy-start.6 = (f32[2,3,3,128,128]{4,3,2,1,0:T(8,128)S(1)}, f32[2,3,3,128,128]{4,3,2,1,0:T(8,128)}, u32[]{:S(2)}) copy-start(f32[2,3,3,128,128]{4,3,2,1,0:T(8,128)} %param.53) | copy-start | bytes 3538948
  0.7 80.5 %copy-start.7 = (f32[3,3,128,256]{3,2,1,0:T(8,128)S(1)}, f32[3,3,128,256]{3,2,1,0:T(8,128)}, u32[]{:S(2)}) copy-start(f32[3,3,128,256]{3,2,1,0:T(8,128)} %param.45) | copy-start | bytes 3538948
  0.8 80.5 %copy-start.8 = (f32[3,3,128,256]{3,2,1,0:T(8,128)S(1)}, f32[3,3,128,256]{3,2,1,0:T(8,128)}, u32[]{:S(2)}) copy-start(f32[3,3,128,256]{3,2,1,0:T(8,128)} %param.54) | copy-start | bytes 3538948
  0.8 80.5 %copy-start.9 = (f32[256,1024]{1,0:T(8,128)S(1)}, f32[256,1024]{1,0:T(8,128)}, u32[]{:S(2)}) copy-start(f32[256,1024]{1,0:T(8,128)} %refs_20_.1) | copy-start | bytes 3145732
  0.8 80.5 %copy-start.10 = (f32[256,1024]{1,0:T(8,128)S(1)}, f32[256,1024]{1,0:T(8,128)}, u32[]{:S(2)}) copy-start(f32[256,1024]{1,0:T(8,128)} %refs_21_.1) | copy-start | bytes 3145732
  0.8 80.5 %copy-start.11 = (f32[256,1024]{1,0:T(8,128)S(1)}, f32[256,1024]{1,0:T(8,128)}, u32[]{:S(2)}) copy-start(f32[256,1024]{1,0:T(8,128)} %refs_22_.1) | copy-start | bytes 3145732
  0.8 80.5 %copy-start.12 = (f32[128,256]{1,0:T(8,128)S(1)}, f32[128,256]{1,0:T(8,128)}, u32[]{:S(2)}) copy-start(f32[128,256]{1,0:T(8,128)} %refs_17_.1) | copy-start | bytes 393220
  0.8 80.5 %copy-start.13 = (f32[128,256]{1,0:T(8,128)S(1)}, f32[128,256]{1,0:T(8,128)}, u32[]{:S(2)}) copy-start(f32[128,256]{1,0:T(8,128)} %refs_18_.1) | copy-start | bytes 393220
  0.8 80.5 %copy-start.14 = (f32[128,256]{1,0:T(8,128)S(1)}, f32[128,256]{1,0:T(8,128)}, u32[]{:S(2)}) copy-start(f32[128,256]{1,0:T(8,128)} %refs_19_.1) | copy-start | bytes 393220
  0.8 80.5 %copy-start.15 = (f32[3,3,256,3]{2,3,1,0:T(4,128)S(1)}, f32[3,3,256,3]{2,3,1,0:T(4,128)}, u32[]{:S(2)}) copy-start(f32[3,3,256,3]{2,3,1,0:T(4,128)} %param.40) | copy-start | bytes 82948
  0.8 80.5 %copy-start.16 = (f32[3,3,256,3]{2,3,1,0:T(4,128)S(1)}, f32[3,3,256,3]{2,3,1,0:T(4,128)}, u32[]{:S(2)}) copy-start(f32[3,3,256,3]{2,3,1,0:T(4,128)} %param.49) | copy-start | bytes 82948
  0.8 80.5 %copy-start.17 = (f32[3,3,256,3]{2,3,1,0:T(4,128)S(1)}, f32[3,3,256,3]{2,3,1,0:T(4,128)}, u32[]{:S(2)}) copy-start(f32[3,3,256,3]{2,3,1,0:T(4,128)} %param.58) | copy-start | bytes 82948
  0.9 80.5 %copy-start.18 = (f32[8,384]{1,0:T(8,128)S(1)}, f32[8,384]{1,0:T(8,128)}, u32[]{:S(2)}) copy-start(f32[8,384]{1,0:T(8,128)} %refs_32_.1) | copy-start | bytes 36868
  0.9 80.5 %copy-start.19 = (f32[8,384]{1,0:T(8,128)S(1)}, f32[8,384]{1,0:T(8,128)}, u32[]{:S(2)}) copy-start(f32[8,384]{1,0:T(8,128)} %refs_33_.1) | copy-start | bytes 36868
  0.9 80.5 %copy-start.20 = (f32[8,384]{1,0:T(8,128)S(1)}, f32[8,384]{1,0:T(8,128)}, u32[]{:S(2)}) copy-start(f32[8,384]{1,0:T(8,128)} %refs_34_.1) | copy-start | bytes 36868
  0.9 80.5 %copy-start.21 = (f32[6,256]{1,0:T(8,128)S(1)}, f32[6,256]{1,0:T(8,128)}, u32[]{:S(2)}) copy-start(f32[6,256]{1,0:T(8,128)} %refs_29_.1) | copy-start | bytes 18436
  0.9 80.5 %copy-start.22 = (f32[6,256]{1,0:T(8,128)S(1)}, f32[6,256]{1,0:T(8,128)}, u32[]{:S(2)}) copy-start(f32[6,256]{1,0:T(8,128)} %refs_30_.1) | copy-start | bytes 18436
  0.9 80.5 %copy-start.23 = (f32[6,256]{1,0:T(8,128)S(1)}, f32[6,256]{1,0:T(8,128)}, u32[]{:S(2)}) copy-start(f32[6,256]{1,0:T(8,128)} %refs_31_.1) | copy-start | bytes 18436
  0.9 80.5 %copy-start.24 = (f32[6,128]{1,0:T(8,128)S(1)}, f32[6,128]{1,0:T(8,128)}, u32[]{:S(2)}) copy-start(f32[6,128]{1,0:T(8,128)} %refs_26_.1) | copy-start | bytes 9220
  0.9 80.4 %copy-start.25 = (f32[6,128]{1,0:T(8,128)S(1)}, f32[6,128]{1,0:T(8,128)}, u32[]{:S(2)}) copy-start(f32[6,128]{1,0:T(8,128)} %refs_27_.1) | copy-start | bytes 9220
  1.0 80.4 %copy-start.26 = (f32[6,128]{1,0:T(8,128)S(1)}, f32[6,128]{1,0:T(8,128)}, u32[]{:S(2)}) copy-start(f32[6,128]{1,0:T(8,128)} %refs_28_.1) | copy-start | bytes 9220

commit v6 on v5

--- a/solution.py
+++ b/solution.py
@@ -944,18 +944,23 @@
     "conv_d": ("attn",),
     "gn_d": ("small",),
     "down": ("down",),
-    "t0a0": ("wide", "small",),
-    "t0a1": ("down", "attn",),
-    "pair_b": ("pair_b", "attn",),
-    "b1i0a": ("wide", "small", "pair_b",),
-    "b1i1a": ("attn",),
-    "pair_a": ("pair_a", "down",),
-    "b0c": ("wide", "small", "pair_b", "pair_a",),
+    "t0a0": ("small", "wide",),
+    "t0a1": ("attn", "down",),
+    "t0b1": ("small",),
+    "t1b1": ("attn",),
+    "pair_b": ("pair_b",),
+    "b1c": ("small", "wide",),
+    "b1i0a": ("pair_b",),
+    "b1i0": ("attn",),
+    "b1i1a": ("down",),
+    "b1i1": ("small",),
+    "pair_a": ("pair_a",),
+    "b0c0": ("wide", "pair_b",),
+    "b0i0": ("pair_a", "down",),
     "end": (
-        "late", "down", "attn", "late", "pair_a", "wide", "attn", "small",
-        "pair_b", "late", "down", "pair_a", "pair_b", "late", "wide", "small",
-        "pair_a", "wide", "small", "down", "down", "pair_b", "pair_b", "pair_a",
-        "pair_a",
+        "late", "small", "attn", "wide", "late", "small", "pair_b", "attn",
+        "pair_a", "down", "pair_b", "pair_a", "wide", "late", "pair_a", "wide",
+        "down", "late", "down", "pair_b", "pair_b", "pair_a", "pair_a",
     ),
 }
 

time: 89.7 us -> 89.5 us (level)
  no operation moved by 1% of the time
where the time goes in v6:
time: 89.5 us; the launch traced here: 89.3 us
  Pallas kernels  87.9 us (98%)
  between operations  1.27 us (1%)
    pallas_call x1, Pallas kernels, main_call(): pl.pallas_call(functools.partial(main_kernel, dp_size), out_shape=[jax.Sh...  80 us
    pallas_call x1, Pallas kernels, update_call(): pl.pallas_call(functools.partial(update_kernel, devices), out_shape=[jax....  7.97 us

profile of v6, /device:TPU:0, one launch (start us, length us, event | category | flops | bytes accessed | tf_op | source)
XLA Modules:
  0.0 89.3 jit_solution(13340911712981351587)
XLA Ops:
  0.7 0.0 copy-start
  0.7 0.0 copy-start.1
  0.7 0.0 copy-start.2
  0.7 0.0 copy-start.3
  0.7 0.0 copy-start.4
  0.7 0.0 copy-start.5
  0.7 0.0 copy-start.6
  0.7 0.0 copy-start.7
  0.8 0.0 copy-start.8
  0.8 0.0 copy-start.9
  0.8 0.0 copy-start.10
  0.8 0.0 copy-start.11
  0.8 0.0 copy-start.12
  0.8 0.0 copy-start.13
  0.8 0.0 copy-start.14
  0.8 0.0 copy-start.15
  0.8 0.0 copy-start.16
  0.8 0.0 copy-start.17
  0.9 0.0 copy-start.18
  0.9 0.0 copy-start.19
  0.9 0.0 copy-start.20
  0.9 0.0 copy-start.21
  0.9 0.0 copy-start.22
  0.9 0.0 copy-start.23
  0.9 0.0 copy-start.24
  0.9 0.0 copy-start.25
  1.0 0.0 copy-start.26
  1.0 80.0 %shard_map.518 = (s16[2560,128]{1,0:T(8,128)(2,1)S(1)}, s16[5120,128]{1,0:T(8,128)(2,1)S(1)}, s16[3072,128]{1,0:T(8,128)(2,1)S(1)}, s16[2048,128]{1,0:T(8,128)(2...) custom-call(s32[4]{0:T(128)} %buckets.1, ...), custom_call_target="tpu_custom_call" | custom-call | flops 8000000000 | bytes 12000000 | tf_op jit(solution)/shard_map/pallas_call | solution.py:927
  80.9 0.0 copy-done
  80.9 0.0 copy-done.1
  80.9 0.0 copy-done.2
  81.0 0.0 copy-done.3
  81.0 0.0 copy-done.4
  81.0 0.0 copy-done.5
  81.0 0.0 copy-done.6
  81.0 0.0 copy-done.7
  81.0 0.0 copy-done.8
  81.0 0.0 copy-done.9
  81.0 0.0 copy-done.10
  81.0 0.0 copy-done.11
  81.0 0.0 copy-done.12
  81.1 0.0 copy-done.13
  81.1 0.0 copy-done.14
  81.1 0.0 copy-done.15
  81.1 0.0 copy-done.16
  81.1 0.0 copy-done.17
  81.1 0.0 copy-done.18
  81.2 8.0 %shard_map.519 = (f32[2304,128]{1,0:T(8,128)}, f32[2304,128]{1,0:T(8,128)}, f32[2304,128]{1,0:T(8,128)}, f32[1152,256]{1,0:T(8,128)}, f32[1152,256]{1,0:T(8,128)...) custom-call(s16[2560,128]{1,0:T(8,128)(2,1)S(1)} %get-tuple-element., ...), custom_call_target="tpu_custom_call" | custom-call | flops 30000000 | bytes 40000000 | tf_op jit(solution)/shard_map/pallas_call | solution.py:1359
  (8 shorter events, 0.0 us)
Async XLA Ops:
  0.7 80.2 %copy-start = (f32[3,3,256,256]{3,2,1,0:T(8,128)S(1)}, f32[3,3,256,256]{3,2,1,0:T(8,128)}, u32[]{:S(2)}) copy-start(f32[3,3,256,256]{3,2,1,0:T(8,128)} %param.37) | copy-start | bytes 7077892
  0.7 80.2 %copy-start.1 = (f32[3,3,256,256]{3,2,1,0:T(8,128)S(1)}, f32[3,3,256,256]{3,2,1,0:T(8,128)}, u32[]{:S(2)}) copy-start(f32[3,3,256,256]{3,2,1,0:T(8,128)} %param.46) | copy-start | bytes 7077892
  0.7 80.2 %copy-start.2 = (f32[3,3,256,256]{3,2,1,0:T(8,128)S(1)}, f32[3,3,256,256]{3,2,1,0:T(8,128)}, u32[]{:S(2)}) copy-start(f32[3,3,256,256]{3,2,1,0:T(8,128)} %param.55) | copy-start | bytes 7077892
  0.7 80.2 %copy-start.3 = (f32[2,3,3,128,128]{4,3,2,1,0:T(8,128)S(1)}, f32[2,3,3,128,128]{4,3,2,1,0:T(8,128)}, u32[]{:S(2)}) copy-start(f32[2,3,3,128,128]{4,3,2,1,0:T(8,128)} %param.35) | copy-start | bytes 3538948
  0.7 80.2 %copy-start.4 = (f32[3,3,128,256]{3,2,1,0:T(8,128)S(1)}, f32[3,3,128,256]{3,2,1,0:T(8,128)}, u32[]{:S(2)}) copy-start(f32[3,3,128,256]{3,2,1,0:T(8,128)} %param.36) | copy-start | bytes 3538948
  0.7 80.2 %copy-start.5 = (f32[2,3,3,128,128]{4,3,2,1,0:T(8,128)S(1)}, f32[2,3,3,128,128]{4,3,2,1,0:T(8,128)}, u32[]{:S(2)}) copy-start(f32[2,3,3,128,128]{4,3,2,1,0:T(8,128)} %param.44) | copy-start | bytes 3538948
  0.7 80.2 %copy-start.6 = (f32[2,3,3,128,128]{4,3,2,1,0:T(8,128)S(1)}, f32[2,3,3,128,128]{4,3,2,1,0:T(8,128)}, u32[]{:S(2)}) copy-start(f32[2,3,3,128,128]{4,3,2,1,0:T(8,128)} %param.53) | copy-start | bytes 3538948
  0.7 80.2 %copy-start.7 = (f32[3,3,128,256]{3,2,1,0:T(8,128)S(1)}, f32[3,3,128,256]{3,2,1,0:T(8,128)}, u32[]{:S(2)}) copy-start(f32[3,3,128,256]{3,2,1,0:T(8,128)} %param.45) | copy-start | bytes 3538948
  0.8 80.2 %copy-start.8 = (f32[3,3,128,256]{3,2,1,0:T(8,128)S(1)}, f32[3,3,128,256]{3,2,1,0:T(8,128)}, u32[]{:S(2)}) copy-start(f32[3,3,128,256]{3,2,1,0:T(8,128)} %param.54) | copy-start | bytes 3538948
  0.8 80.2 %copy-start.9 = (f32[256,1024]{1,0:T(8,128)S(1)}, f32[256,1024]{1,0:T(8,128)}, u32[]{:S(2)}) copy-start(f32[256,1024]{1,0:T(8,128)} %refs_20_.1) | copy-start | bytes 3145732
  0.8 80.2 %copy-start.10 = (f32[256,1024]{1,0:T(8,128)S(1)}, f32[256,1024]{1,0:T(8,128)}, u32[]{:S(2)}) copy-start(f32[256,1024]{1,0:T(8,128)} %refs_21_.1) | copy-start | bytes 3145732
  0.8 80.2 %copy-start.11 = (f32[256,1024]{1,0:T(8,128)S(1)}, f32[256,1024]{1,0:T(8,128)}, u32[]{:S(2)}) copy-start(f32[256,1024]{1,0:T(8,128)} %refs_22_.1) | copy-start | bytes 3145732
  0.8 80.2 %copy-start.12 = (f32[128,256]{1,0:T(8,128)S(1)}, f32[128,256]{1,0:T(8,128)}, u32[]{:S(2)}) copy-start(f32[128,256]{1,0:T(8,128)} %refs_17_.1) | copy-start | bytes 393220
  0.8 80.2 %copy-start.13 = (f32[128,256]{1,0:T(8,128)S(1)}, f32[128,256]{1,0:T(8,128)}, u32[]{:S(2)}) copy-start(f32[128,256]{1,0:T(8,128)} %refs_18_.1) | copy-start | bytes 393220
  0.8 80.2 %copy-start.14 = (f32[128,256]{1,0:T(8,128)S(1)}, f32[128,256]{1,0:T(8,128)}, u32[]{:S(2)}) copy-start(f32[128,256]{1,0:T(8,128)} %refs_19_.1) | copy-start | bytes 393220
  0.8 80.2 %copy-start.15 = (f32[3,3,256,3]{2,3,1,0:T(4,128)S(1)}, f32[3,3,256,3]{2,3,1,0:T(4,128)}, u32[]{:S(2)}) copy-start(f32[3,3,256,3]{2,3,1,0:T(4,128)} %param.40) | copy-start | bytes 82948
  0.8 80.2 %copy-start.16 = (f32[3,3,256,3]{2,3,1,0:T(4,128)S(1)}, f32[3,3,256,3]{2,3,1,0:T(4,128)}, u32[]{:S(2)}) copy-start(f32[3,3,256,3]{2,3,1,0:T(4,128)} %param.49) | copy-start | bytes 82948
  0.8 80.2 %copy-start.17 = (f32[3,3,256,3]{2,3,1,0:T(4,128)S(1)}, f32[3,3,256,3]{2,3,1,0:T(4,128)}, u32[]{:S(2)}) copy-start(f32[3,3,256,3]{2,3,1,0:T(4,128)} %param.58) | copy-start | bytes 82948
  0.9 80.2 %copy-start.18 = (f32[8,384]{1,0:T(8,128)S(1)}, f32[8,384]{1,0:T(8,128)}, u32[]{:S(2)}) copy-start(f32[8,384]{1,0:T(8,128)} %refs_32_.1) | copy-start | bytes 36868
  0.9 80.2 %copy-start.19 = (f32[8,384]{1,0:T(8,128)S(1)}, f32[8,384]{1,0:T(8,128)}, u32[]{:S(2)}) copy-start(f32[8,384]{1,0:T(8,128)} %refs_33_.1) | copy-start | bytes 36868
  0.9 80.2 %copy-start.20 = (f32[8,384]{1,0:T(8,128)S(1)}, f32[8,384]{1,0:T(8,128)}, u32[]{:S(2)}) copy-start(f32[8,384]{1,0:T(8,128)} %refs_34_.1) | copy-start | bytes 36868
  0.9 80.2 %copy-start.21 = (f32[6,256]{1,0:T(8,128)S(1)}, f32[6,256]{1,0:T(8,128)}, u32[]{:S(2)}) copy-start(f32[6,256]{1,0:T(8,128)} %refs_29_.1) | copy-start | bytes 18436
  0.9 80.2 %copy-start.22 = (f32[6,256]{1,0:T(8,128)S(1)}, f32[6,256]{1,0:T(8,128)}, u32[]{:S(2)}) copy-start(f32[6,256]{1,0:T(8,128)} %refs_30_.1) | copy-start | bytes 18436
  0.9 80.2 %copy-start.23 = (f32[6,256]{1,0:T(8,128)S(1)}, f32[6,256]{1,0:T(8,128)}, u32[]{:S(2)}) copy-start(f32[6,256]{1,0:T(8,128)} %refs_31_.1) | copy-start | bytes 18436
  0.9 80.2 %copy-start.24 = (f32[6,128]{1,0:T(8,128)S(1)}, f32[6,128]{1,0:T(8,128)}, u32[]{:S(2)}) copy-start(f32[6,128]{1,0:T(8,128)} %refs_26_.1) | copy-start | bytes 9220
  0.9 80.2 %copy-start.25 = (f32[6,128]{1,0:T(8,128)S(1)}, f32[6,128]{1,0:T(8,128)}, u32[]{:S(2)}) copy-start(f32[6,128]{1,0:T(8,128)} %refs_27_.1) | copy-start | bytes 9220
  1.0 80.2 %copy-start.26 = (f32[6,128]{1,0:T(8,128)S(1)}, f32[6,128]{1,0:T(8,128)}, u32[]{:S(2)}) copy-start(f32[6,128]{1,0:T(8,128)} %refs_28_.1) | copy-start | bytes 9220
